TPU v7x, 32 devices: a whole 2x2x4 slice. The times are simulated.
32 devices in a mesh: grp: 2 (over x), suf: 4 (over y, core), head: 4 (over z).
Axes of the slice: x: 2, y: 2, z: 4, core: 2. Of those that a mesh axis runs over, the one named last changes fastest.
Arguments:
- prefix_x: bfloat16 [1024, 8192], P(('grp', 'suf'), 'head'), parts along dimension 0, may hold values from -6 to 6
- prefix_b: bfloat16 [1024, 1024], P(('grp', 'suf'), 'head'), parts along dimension 0, may hold values from -6 to 6
- prefix_c: bfloat16 [1024, 1024], P(('grp', 'suf'), 'head'), parts along dimension 0, may hold values from -6 to 6
- prefix_dt: float32 [128, 1024], P('head', ('grp', 'suf')), parts along dimension 1, may hold values from -3 to 3
- prefix_grad: bfloat16 [1024, 8192], P(('grp', 'suf'), 'head'), parts along dimension 0, may hold values from -0.59765625 to 0.59765625
- suffix_x: bfloat16 [8, 128, 8192], P(('grp', 'suf'), None, 'head'), parts along dimension 0, may hold values from -6 to 6
- suffix_b: bfloat16 [8, 128, 1024], P(('grp', 'suf'), None, 'head'), parts along dimension 0, may hold values from -6 to 6
- suffix_c: bfloat16 [8, 128, 1024], P(('grp', 'suf'), None, 'head'), parts along dimension 0, may hold values from -6 to 6
- suffix_dt: float32 [128, 8, 128], P('head', ('grp', 'suf')), parts along dimension 1, may hold values from -3 to 3
- suffix_grad: bfloat16 [8, 128, 8192], P(('grp', 'suf'), None, 'head'), parts along dimension 0, may hold values from -0.59765625 to 0.59765625
- lengths: int32 [8], P(('grp', 'suf')), parts along dimension 0, may hold values from 1 to 128, 384 in all
- loss_mask: int32 [8, 128], P(('grp', 'suf')), parts along dimension 0, may hold values 0 or 1
- advantage: float32 [8], P(('grp', 'suf')), parts along dimension 0, may hold values from -3 to 3
- conv_x: bfloat16 [4, 8192], P(None, 'head'), may hold values from -3 to 3
- conv_b: bfloat16 [4, 1024], P(None, 'head'), may hold values from -3 to 3
- conv_c: bfloat16 [4, 1024], P(None, 'head'), may hold values from -3 to 3
- decay_rate: float32 [128], P('head'), may hold values from 7.8125e-05 to 0.05
- dt_bias: float32 [128], P('head'), may hold values from -1 to 0.5
- skip: float32 [128], P('head'), may hold values from 0.5 to 1.5
Outputs:
- prefix_dx: bfloat16 [1024, 8192], P(('grp', 'suf'), 'head'), parts along dimension 0
- prefix_db: bfloat16 [1024, 1024], P(('grp', 'suf'), 'head'), parts along dimension 0
- prefix_dc: bfloat16 [1024, 1024], P(('grp', 'suf'), 'head'), parts along dimension 0
- prefix_ddt: float32 [128, 1024], P('head', ('grp', 'suf')), parts along dimension 1
- suffix_dx: bfloat16 [8, 128, 8192], P(('grp', 'suf'), None, 'head'), parts along dimension 0
- suffix_db: bfloat16 [8, 128, 1024], P(('grp', 'suf'), None, 'head'), parts along dimension 0
- suffix_dc: bfloat16 [8, 128, 1024], P(('grp', 'suf'), None, 'head'), parts along dimension 0
- suffix_ddt: float32 [128, 8, 128], P('head', ('grp', 'suf')), parts along dimension 1
There are 2 independent parts, one for each index of `grp`. A program takes and returns all parts, laid end to end along the dimension named above; an argument that names none is the same for every part. Nothing has to cross between parts.
Inputs may be any that keep to these rules, and one draw needn't show every extreme that they name: `lengths`: some suffix has exactly 128 tokens.
All inputs are finite; a program needn't handle non-finite values. No bound on the sum of `lengths` or of `loss_mask` on one device may be relied on, other than what follows from the above.
Results may differ from a plain program's by a relative error of at most 0.001.
Values may be sent and summed in bfloat16 or wider, within the bound.
A program may use at most 128 MiB of HBM per device.

v0:
```python
import functools

import jax
import jax.numpy as jnp
from jax import lax
from jax.experimental import pallas as pl
from jax.experimental.pallas import tpu as pltpu
from jax.sharding import PartitionSpec as P

HD = 64
N = 128
KW = 4
Q = 128
F32 = jnp.float32
BF16 = jnp.bfloat16
EXACT = lax.Precision.HIGHEST
MESH = pl.DeviceIdType.MESH
NN = (((1,), (0,)), ((), ()))
NT = (((1,), (1,)), ((), ()))


def mm(a, b, dims=NN):
    return lax.dot_general(a, b, dims, preferred_element_type=F32)


def split(a):
    hi = a.astype(BF16)
    return hi, (a - hi.astype(F32)).astype(BF16)


def mm3(a, b, dims=NN):
    ah, al = a
    bh, bl = b
    axis = dims[0][1][0]
    return mm(
        jnp.concatenate([ah, ah, al], axis=1), jnp.concatenate([bh, bl, bh], axis=axis), dims
    )


def conv_pre(halo, u, taps):
    w = jnp.concatenate([halo.astype(F32), u.astype(F32)], axis=0)
    taps = taps.astype(F32)
    out = w[5 : 5 + Q] * taps[0:1]
    for k in range(1, KW):
        out = out + w[5 + k : 5 + k + Q] * taps[k : k + 1]
    return out


def silu(v):
    return v * jax.nn.sigmoid(v)


def conv_back(dact, pre, taps):
    taps = taps.astype(F32)
    sig = jax.nn.sigmoid(pre)
    dpre = dact * (sig * (1.0 + pre * (1.0 - sig)))
    zero = jnp.zeros((8, dpre.shape[1]), F32)
    ext = jnp.concatenate([zero, dpre, zero], axis=0)
    du = ext[11 : 11 + Q] * taps[0:1]
    left = ext[8:16] * taps[0:1]
    for k in range(1, KW):
        du = du + ext[11 - k : 11 - k + Q] * taps[k : k + 1]
        left = left + ext[8 - k : 16 - k] * taps[k : k + 1]
    return du, left


def softplus(v):
    return jnp.maximum(v, 0.0) + jnp.log1p(jnp.exp(-jnp.abs(v)))


def tri(transposed=False):
    row = lax.broadcasted_iota(jnp.int32, (Q, Q), 0)
    col = lax.broadcasted_iota(jnp.int32, (Q, Q), 1)
    return (row >= col) if transposed else (row <= col)


def expander(heads):
    row = lax.broadcasted_iota(jnp.int32, (heads, heads * HD), 0)
    col = lax.broadcasted_iota(jnp.int32, (heads, heads * HD), 1)
    return ((col >= row * HD) & (col < (row + 1) * HD)).astype(F32)


def decays(dt_ref, bias_ref, rate_ref):
    raw = dt_ref[...] + bias_ref[...]
    step = softplus(raw)
    cum = lax.dot_general(
        -step * rate_ref[...], tri().astype(F32), NN, precision=EXACT, preferred_element_type=F32
    )
    return raw, step, cum


def widen(rows, spread):
    return lax.dot_general(rows.T, spread, NN, precision=EXACT, preferred_element_type=F32)


def row_weight(len_ref, adv_ref, mask_ref):
    at = lax.broadcasted_iota(jnp.int32, (1, Q), 1)
    inside = (at < len_ref[0]).astype(F32)
    return adv_ref[0] * mask_ref[...].astype(F32) * inside


def states_kernel(
    len_ref, adv_ref, mask_ref,
    px, pb, pc, pdt, pg, phx, phb, phc,
    sx, sb, sc, sdt, sg, shx, shb, shc,
    tx, tb, tc, rate, bias, skip,
    own_ref, adj_ref, suf_ref, dec_ref,
):
    heads = pdt.shape[0]
    spread = expander(heads)
    raw, step, cum = decays(pdt, bias, rate)
    last = cum[:, Q - 1 : Q]
    push = widen(jnp.exp(last - cum) * step, spread)
    pull = jnp.exp(cum)
    pull_wide = widen(pull, spread)
    dec_ref[...] = jnp.broadcast_to(pull_wide[Q - 1 : Q], dec_ref.shape)
    b_t = split(silu(conv_pre(phb[...], pb[...], tb[...])).T)
    c_t = split(silu(conv_pre(phc[...], pc[...], tc[...])).T)
    x_act = silu(conv_pre(phx[...], px[...], tx[...]))
    own_ref[...] = mm3(b_t, split(x_act * push))
    adj_ref[...] = mm3(c_t, split(pg[...].astype(F32) * pull_wide))
    s_raw, s_step, s_cum = decays(sdt, bias, rate)
    weight = row_weight(len_ref, adv_ref, mask_ref)
    s_pull = widen(jnp.exp(s_cum) * weight, spread)
    sc_t = split(silu(conv_pre(shc[...], sc[...], tc[...])).T)
    suf_ref[...] = mm3(sc_t, split(sg[...].astype(F32) * s_pull))


def within(x_ref, b_ref, c_ref, dt_ref, g_ref, hx, hb, hc, tx, tb, tc, rate, bias, weight,
           dx_out, db_out, dc_out, r_out):
    heads = dt_ref.shape[0]
    raw, step, cum = decays(dt_ref, bias, rate)
    cum_col = cum.T
    step_col = step.T
    b_act = split(silu(conv_pre(hb[...], b_ref[...], tb[...])))
    c_act = split(silu(conv_pre(hc[...], c_ref[...], tc[...])))
    bc = mm3(b_act, c_act, NT)
    keep = tri()
    lane = lax.broadcasted_iota(jnp.int32, (Q, 2 * HD), 1)
    total = jnp.zeros((Q, Q), F32)
    width = heads * HD
    chunk = min(width, 2 * HD)
    for at in range(0, width, chunk):
        cols = slice(at, at + chunk)
        x_act = silu(conv_pre(hx[:, cols], x_ref[:, cols], tx[:, cols]))
        grad = g_ref[:, cols]
        xh, xl = split(x_act)
        twice = jnp.concatenate([grad, grad], axis=1)
        left, right = [], []
        for k in range(chunk // HD):
            h = at // HD + k
            if chunk == HD:
                xhm, xlm, gm = xh, xl, grad
            else:
                mine = (lane >= k * HD) & (lane < (k + 1) * HD)
                zero = jnp.zeros((), BF16)
                xhm = jnp.where(mine, xh, zero)
                xlm = jnp.where(mine, xl, zero)
                gm = jnp.where(mine, grad, zero)
            gap = jnp.where(keep, cum[h : h + 1] - cum_col[:, h : h + 1], -1e30)
            att = jnp.exp(gap) * step_col[:, h : h + 1]
            if weight is not None:
                att = att * weight
            dm = mm(jnp.concatenate([xhm, xlm], axis=1), twice, NT)
            q = dm * att
            total = total + q
            r_out[h : h + 1] = jnp.sum(q * bc, axis=0, keepdims=True)
            mh, ml = split(att * bc)
            left += [mh, ml]
            right += [gm, gm]
        dx_out[:, cols] = mm(jnp.concatenate(left, axis=1), jnp.concatenate(right, axis=0))
    db_out[...] = mm3(split(total), c_act)
    dc_out[...] = mm3(split(total.T), b_act)


def within_kernel(
    len_ref, adv_ref, mask_ref,
    px, pb, pc, pdt, pg, phx, phb, phc,
    sx, sb, sc, sdt, sg, shx, shb, shc,
    tx, tb, tc, rate, bias, skip,
    p_dx, p_db, p_dc, p_r, s_dx, s_db, s_dc, s_r,
):
    within(px, pb, pc, pdt, pg, phx, phb, phc, tx, tb, tc, rate, bias, None, p_dx, p_db, p_dc, p_r)
    weight = row_weight(len_ref, adv_ref, mask_ref)
    within(sx, sb, sc, sdt, sg, shx, shb, shc, tx, tb, tc, rate, bias, weight, s_dx, s_db, s_dc, s_r)


def per_head(spread, value):
    hi, lo = split(value)
    e = spread.astype(BF16)
    return mm(e, hi, NT) + mm(e, lo, NT)


def carried(x_ref, b_ref, c_ref, dt_ref, g_ref, hx, hb, hc, tx, tb, tc, rate, bias, skip, weight,
            start, adjoint, in_dx, in_db, in_dc, in_r, dx, db, dc, ddt, lx, lb, lc, tails):
    heads = dt_ref.shape[0]
    spread = expander(heads)
    raw, step, cum = decays(dt_ref, bias, rate)
    pull = jnp.exp(cum)
    if weight is not None:
        pull = pull * weight
    pull_wide = widen(pull, spread)
    gain = skip[...] if weight is None else skip[...] * weight
    gain_wide = widen(jnp.broadcast_to(gain, (heads, Q)), spread)
    b_pre = conv_pre(hb[...], b_ref[...], tb[...])
    c_pre = conv_pre(hc[...], c_ref[...], tc[...])
    x_pre = conv_pre(hx[...], x_ref[...], tx[...])
    x_act = silu(x_pre)
    grad = g_ref[...].astype(F32)
    c_act = split(silu(c_pre))
    s_split = split(start[...])
    pulled = grad * pull_wide
    across = per_head(spread, pulled * mm3(c_act, s_split))
    dc_act = in_dc[...] + mm3(split(pulled), s_split, NT)
    db_act = in_db[...]
    dx_in = in_dx[...]
    col_sum = per_head(spread, x_act * dx_in)
    end = jnp.zeros((heads, 1), F32)
    if adjoint is not None:
        last = cum[:, Q - 1 : Q]
        push = widen(jnp.exp(last - cum) * step, spread)
        b_act = split(silu(b_pre))
        a_split = split(adjoint[...])
        moved = push * mm3(b_act, a_split)
        dx_in = dx_in + moved
        v = per_head(spread, x_act * moved)
        col_sum = col_sum + v
        db_act = db_act + mm3(split(x_act * push), a_split, NT)
        both = jnp.sum(per_head(spread, start[...] * adjoint[...]), axis=1, keepdims=True)
        end = jnp.sum(v, axis=1, keepdims=True) + jnp.exp(last) * both
    change = in_r[...] + across - col_sum
    dlog = end + lax.dot_general(
        change, tri(True).astype(F32), NN, precision=EXACT, preferred_element_type=F32
    )
    ddt[...] = (col_sum / step - rate[...] * dlog) * jax.nn.sigmoid(raw)
    for dact, pre, taps, out, left, tail in (
        (dx_in + gain_wide * grad, x_pre, tx, dx, lx, 0),
        (db_act, b_pre, tb, db, lb, 1),
        (dc_act, c_pre, tc, dc, lc, 2),
    ):
        du, dleft = conv_back(dact, pre, taps[...])
        out[...] = du.astype(BF16)
        left[...] = dleft
        if tails is not None:
            tails[tail][...] = du[Q - 8 :]


def carried_kernel(
    len_ref, adv_ref, mask_ref,
    px, pb, pc, pdt, pg, phx, phb, phc,
    sx, sb, sc, sdt, sg, shx, shb, shc,
    tx, tb, tc, rate, bias, skip,
    p_start, p_adj, s_start,
    p_idx, p_idb, p_idc, p_r, s_idx, s_idb, s_idc, s_r,
    p_dx, p_db, p_dc, p_ddt, s_dx, s_db, s_dc, s_ddt,
    plx, plb, plc, slx, slb, slc, ptx, ptb, ptc,
):
    carried(px, pb, pc, pdt, pg, phx, phb, phc, tx, tb, tc, rate, bias, skip, None,
            p_start, p_adj, p_idx, p_idb, p_idc, p_r, p_dx, p_db, p_dc, p_ddt,
            plx, plb, plc, (ptx, ptb, ptc))
    weight = row_weight(len_ref, adv_ref, mask_ref)
    carried(sx, sb, sc, sdt, sg, shx, shb, shc, tx, tb, tc, rate, bias, skip, weight,
            s_start, None, s_idx, s_idb, s_idc, s_r, s_dx, s_db, s_dc, s_ddt,
            slx, slb, slc, None)


def gather_kernel(ways, x_ref, out_ref, send, recv, own):
    me = lax.axis_index("suf")
    barrier = pltpu.get_barrier_semaphore()
    for d in range(1, ways):
        pl.semaphore_signal(
            barrier, inc=1, device_id={"suf": lax.rem(me + d, ways)}, device_id_type=MESH
        )
    pl.semaphore_wait(barrier, ways - 1)
    copies = []
    for d in range(1, ways):
        copies.append(
            pltpu.make_async_remote_copy(
                src_ref=x_ref,
                dst_ref=out_ref.at[d],
                send_sem=send.at[d],
                recv_sem=recv.at[d],
                device_id={"suf": lax.rem(me + d, ways)},
                device_id_type=MESH,
            )
        )
        copies[-1].start()
    mine = pltpu.make_async_copy(x_ref, out_ref.at[0], own)
    mine.start()
    mine.wait()
    for copy in copies:
        copy.wait()


def gather_small(block, ways, ident):
    if ways == 1:
        return block[None]
    return pl.pallas_call(
        functools.partial(gather_kernel, ways),
        out_shape=jax.ShapeDtypeStruct((ways,) + block.shape, block.dtype),
        in_specs=[pl.BlockSpec(memory_space=pltpu.VMEM)],
        out_specs=pl.BlockSpec(memory_space=pltpu.VMEM),
        scratch_shapes=[
            pltpu.SemaphoreType.DMA((ways,)),
            pltpu.SemaphoreType.DMA((ways,)),
            pltpu.SemaphoreType.DMA,
        ],
        compiler_params=pltpu.CompilerParams(collective_id=ident, has_side_effects=True),
    )(block)


def exchange(parts, bit, ways):
    route = [(i, i ^ bit) for i in range(ways)]
    return [lax.ppermute(part, "suf", route) for part in parts]


def combine(own, adj, suf, dec, ways):
    me = lax.axis_index("suf")
    start = jnp.zeros_like(own)
    before = jnp.ones_like(dec)
    tail = jnp.zeros_like(adj)
    after = jnp.ones_like(dec)
    bit = 1
    while bit < ways:
        upper = (me & bit) != 0
        final = bit * 2 == ways
        if final:
            second = jnp.where(upper, adj + dec * suf, suf)
            own_, second_, dec_ = exchange((own, second, dec), bit, ways)
            start = jnp.where(upper, before * own_ + start, start)
            end = jnp.where(upper, dec * own_ + own, dec_ * own + own_)
            total = suf + second_
            tail = jnp.where(
                upper, tail + after * total, tail + after * (second_ + dec_ * suf)
            )
            return start, end, tail
        own_, adj_, suf_, dec_ = exchange((own, adj, suf, dec), bit, ways)
        start = jnp.where(upper, before * own_ + start, start)
        before = jnp.where(upper, before * dec_, before)
        tail = jnp.where(upper, tail, tail + after * adj_)
        after = jnp.where(upper, after, after * dec_)
        own = jnp.where(upper, dec * own_ + own, dec_ * own + own_)
        adj = jnp.where(upper, adj_ + dec_ * adj, adj + dec * adj_)
        suf = suf + suf_
        dec = dec * dec_
        bit *= 2
    return start, own, tail + after * suf


def shards(
    prefix_x, prefix_b, prefix_c, prefix_dt, prefix_grad,
    suffix_x, suffix_b, suffix_c, suffix_dt, suffix_grad,
    lengths, loss_mask, advantage, conv_x, conv_b, conv_c, decay_rate, dt_bias, skip,
):
    ways = lax.axis_size("suf")
    me = lax.axis_index("suf")
    heads = decay_rate.shape[0]
    groups = conv_b.shape[1] // N
    per = heads // groups
    wide = per * HD
    full = heads * HD
    nb = groups * N
    margin = KW - 1

    tails = jnp.concatenate([prefix_x[-16:], prefix_b[-16:], prefix_c[-16:]], axis=1)
    gathered = gather_small(tails, ways, 0)[:, 8:]
    left = jnp.where(me == 0, jnp.zeros_like(gathered[0]), gathered[1 % ways])
    context = lax.dynamic_index_in_dim(gathered, lax.rem(me + 1, ways), 0, False)

    def cut(block):
        return block[:, :full], block[:, full : full + nb], block[:, full + nb :]

    sm = pl.BlockSpec(memory_space=pltpu.SMEM)
    sx = pl.BlockSpec((Q, wide), lambda g: (0, g))
    sb = pl.BlockSpec((Q, N), lambda g: (0, g))
    sdt = pl.BlockSpec((per, Q), lambda g: (g, 0))
    hx = pl.BlockSpec((8, wide), lambda g: (0, g))
    hb = pl.BlockSpec((8, N), lambda g: (0, g))
    kx = pl.BlockSpec((KW, wide), lambda g: (0, g))
    kb = pl.BlockSpec((KW, N), lambda g: (0, g))
    ph = pl.BlockSpec((per, 1), lambda g: (g, 0))
    half = [sx, sb, sb, sdt, sx, hx, hb, hb]
    base_specs = (
        [sm, sm, pl.BlockSpec((1, Q), lambda g: (0, 0))] + half + half + [kx, kb, kb, ph, ph, ph]
    )
    base = (
        (lengths, advantage, loss_mask)
        + (prefix_x, prefix_b, prefix_c, prefix_dt, prefix_grad)
        + cut(left)
        + (suffix_x[0], suffix_b[0], suffix_c[0], suffix_dt[:, 0], suffix_grad[0])
        + cut(context)
        + (conv_x, conv_b, conv_c, decay_rate[:, None], dt_bias[:, None], skip[:, None])
    )

    def shape(rows, columns, kind=F32):
        return jax.ShapeDtypeStruct((rows, columns), kind)

    params = pltpu.CompilerParams(vmem_limit_bytes=48 * 1024 * 1024)
    state_shape = shape(N, full)
    own, adj, suf, dec = pl.pallas_call(
        states_kernel,
        grid=(groups,),
        in_specs=base_specs,
        out_specs=[sx, sx, sx, hx],
        out_shape=[state_shape] * 3 + [shape(8, full)],
        compiler_params=params,
        name="states",
    )(*base)

    inner_specs = [sx, sb, sb, sdt]
    inner_shape = [shape(Q, full), shape(Q, nb), shape(Q, nb), shape(heads, Q)]
    inner = pl.pallas_call(
        within_kernel,
        grid=(groups,),
        in_specs=base_specs,
        out_specs=inner_specs * 2,
        out_shape=inner_shape * 2,
        compiler_params=params,
        cost_estimate=pl.CostEstimate(
            flops=heads * 2 * 12 * Q * Q * Q, bytes_accessed=6 << 20, transcendentals=heads * Q * Q
        ),
        name="within",
    )(*base)

    start, end, adjoint = combine(own, adj, suf, dec[:1], ways)

    out_specs = [sx, sb, sb, sdt] * 2 + [hx, hb, hb] * 3
    out_shape = [shape(Q, full, BF16), shape(Q, nb, BF16), shape(Q, nb, BF16), shape(heads, Q)] * 2
    out_shape += [shape(8, full), shape(8, nb), shape(8, nb)] * 3
    outs = pl.pallas_call(
        carried_kernel,
        grid=(groups,),
        in_specs=base_specs + [sx, sx, sx] + inner_specs * 2,
        out_specs=out_specs,
        out_shape=out_shape,
        compiler_params=params,
        name="carried",
    )(*base, start, adjoint, end, *inner)

    lefts = jnp.concatenate(outs[8:11], axis=1)[:margin]
    sufs = jnp.concatenate(outs[11:14], axis=1)[:margin]
    pad = jnp.zeros((8 - margin, lefts.shape[1]), F32)
    message = jnp.concatenate([lefts, pad, sufs, pad], axis=0)
    got = gather_small(message, ways, 1)
    extra = jnp.where(
        me == ways - 1, jnp.sum(got[:, 8 : 8 + margin], axis=0), got[ways - 1, :margin]
    )
    finished = []
    for at, add in enumerate(cut(extra)):
        tail = (outs[14 + at][-margin:] + add).astype(BF16)
        finished.append(outs[at].at[-margin:].set(tail))
    return (
        *finished,
        outs[3],
        outs[4][None],
        outs[5][None],
        outs[6][None],
        outs[7][:, None],
    )


def solution(mesh):
    rows = P(("grp", "suf"), "head")
    deep = P(("grp", "suf"), None, "head")
    flat = P("head", ("grp", "suf"))
    flat3 = P("head", ("grp", "suf"), None)
    one = P(("grp", "suf"))
    return jax.shard_map(
        shards,
        mesh=mesh,
        in_specs=(
            rows, rows, rows, flat, rows,
            deep, deep, deep, flat3, deep,
            one, P(("grp", "suf"), None), one,
            P(None, "head"), P(None, "head"), P(None, "head"),
            P("head"), P("head"), P("head"),
        ),
        out_specs=(rows, rows, rows, flat, deep, deep, deep, flat3),
        check_vma=False,
    )
```

profile of v0, /device:TPU:1, one launch (start us, length us, event | category | flops | bytes accessed | tf_op | source)
XLA Modules:
  0.0 126.4 jit_solution(1421977370359778114)
XLA Ops:
  0.7 0.8 slice-done
  1.5 0.6 pad_maximum_fusion.x_ref
  2.1 9.0 %shard_map.242 = bf16[4,16,2560]{2,1,0:T(8,128)(2,1)} custom-call(bf16[16,2560]{1,0:T(8,128)(2,1)} %pad_maximum_fusion.x_ref), custom_call_target="tpu_custom_call" | custom-call | tf_op jit(solution)/shard_map/pallas_call | solution.py:298
  11.1 0.9 slice.125
  12.1 0.8 select_bitcast_fusion
  12.9 0.6 copy-done.30
  15.2 0.6 copy-done.22
  15.8 1.0 copy-done.2
  16.8 1.0 copy-done.4
  17.9 0.7 copy-done.14
  18.6 0.7 copy-done.17
  19.3 6.3 %states.1 = (f32[128,2048]{1,0:T(8,128)S(1)}, f32[128,2048]{1,0:T(8,128)S(1)}, f32[128,2048]{1,0:T(8,128)}, f32[8,2048]{1,0:T(8,128)S(1)}) custom-call(s32[1]{0:T(128)S(6)} %copy.40.len_ref, f32[1]{0:T(128)S(6)} %copy.41.adv_ref, s32[1,128]{1,0:T(1,128)S(1)} %copy-done.26, bf16[128,2048]{1,0:T(8,128)(2,1)S(1)} %copy-done, bf16[128,256]{1,0:T(8,128)(2,1)S(1)} %copy-done.9, ...), custom_call_target="tpu_custom_call" | custom-call | tf_op jit(solution)/shard_map/states/pallas_call | solution.py:400
  26.3 0.6 slice.129
  27.3 4.4 %collective-permute-done = f32[1,2048]{1,0:T(1,128)} collective-permute-done((f32[1,2048]{1,0:T(1,128)}, f32[1,2048]{1,0:T(1,128)}, u32[]{:S(2)}, u32[]{:S(2)}) %collective-permute-start) | collective-permute-done | bytes 8224 | tf_op jit(solution)/shard_map/ppermute | solution.py:314
  31.7 1.5 %broadcast_select_fusion = (f32[1,2048]{1,0:T(1,128)}, f32[1,2048]{1,0:T(1,128)}, f32[1,2048]{1,0:T(1,128)}) fusion(f32[1,2048]{1,0:T(1,128)} %collective-permute-done, pred[]{:T(512)S(6)} %ne.7, f32[8,2048]{1,0:T(8,128)} %copy-done.25), kind=kLoop, calls=%fused_computation.23 | loop fusion | flops 6144 | bytes 40961 | tf_op jit(solution)/shard_map/jit(_where)/select_n | solution.py:341
  33.2 4.7 %add_select_fusion.3 = (f32[128,2048]{1,0:T(8,128)}, f32[128,2048]{1,0:T(8,128)}, f32[128,2048]{1,0:T(8,128)}) fusion(f32[128,2048]{1,0:T(8,128)} %copy-done.8, f32[128,2048]{1,0:T(8,128)} %collective-permute-done.3, f32[2048]{0:T(1024)} %bitcast.14, f32[2048]{0:T(1024)} %bitcast.12, f32[2048]{0:T(1024)} %bitcast.11, pred[]{:T(512)S(6)} %ne.7, pred[]{:T(512)S(6)} %ne.6, ...), kind=kLoop, calls=%fused_computation.3 | loop fusion | flops 3670016 | bytes 9461762 | tf_op jit(solution)/shard_map/jit(_where)/select_n | solution.py:328
  37.9 1.4 %collective-permute-start.2 = (f32[128,2048]{1,0:T(8,128)}, f32[128,2048]{1,0:T(8,128)}, u32[]{:S(2)}, u32[]{:S(2)}) collective-permute-start(f32[128,2048]{1,0:T(8,128)} %get-tuple-element.120), channel_id=1, source_target_pairs={{0,8},{4,12},{8,0},{12,4},{1,9},{5,13},{9,1},{13,5},{2,10},{6,14},... | collective-permute-start | bytes 3145736 | tf_op jit(solution)/shard_map/ppermute | solution.py:314
  39.4 1.4 %collective-permute-start.6 = (f32[1,2048]{1,0:T(1,128)}, f32[1,2048]{1,0:T(1,128)S(1)}, u32[]{:S(2)}, u32[]{:S(2)}) collective-permute-start(f32[1,2048]{1,0:T(1,128)} %get-tuple-element.123), channel_id=1, source_target_pairs={{0,8},{4,12},{8,0},{12,4},{1,9},{5,13},{9,1},{13,5},{2,10},{6,14},... | collective-permute-start | bytes 24584 | tf_op jit(solution)/shard_map/ppermute | solution.py:314
  40.8 7.7 %within.1 = (f32[128,2048]{1,0:T(8,128)S(1)}, f32[128,256]{1,0:T(8,128)S(1)}, f32[128,256]{1,0:T(8,128)S(1)}, f32[32,128]{1,0:T(8,128)S(1)}, f32[128,2048]{1,0:T...) custom-call(s32[1]{0:T(128)S(6)} %copy.40.len_ref, f32[1]{0:T(128)S(6)} %copy.41.adv_ref, ...), custom_call_target="tpu_custom_call" | custom-call | flops 1610612736 | bytes 6291456 | tf_op jit(solution)/shard_map/within/pallas_call | solution.py:412
  48.5 1.0 copy-done.6
  49.5 1.0 copy-done.7
  50.5 35.0 %collective-permute-done.6 = f32[1,2048]{1,0:T(1,128)S(1)} collective-permute-done((f32[1,2048]{1,0:T(1,128)}, f32[1,2048]{1,0:T(1,128)S(1)}, u32[]{:S(2)}, u32[]{:S(2)}) %collective-permute-start.6) | collective-permute-done | bytes 8224 | tf_op jit(solution)/shard_map/ppermute | solution.py:314
  85.6 4.1 %add_select_fusion.1 = (f32[128,2048]{1,0:T(8,128)}, f32[128,2048]{1,0:T(8,128)S(1)}, f32[128,2048]{1,0:T(8,128)S(1)}) fusion(f32[128,2048]{1,0:T(8,128)} %collective-permute-done.2, f32[128,2048]{1,0:T(8,128)} %get-tuple-element.120, f32[2048]{0:T(1024)S(1)} %bitcast.43, f32[2048]{0:T(1024)} %bitcast.14, pred[]{:T(512)S(6)} %ne.6, ...), kind=kLoop, calls=%fused_computation.1 | loop fusion | flops 4718592 | bytes 9469954 | tf_op jit(solution)/shard_map/jit(_where)/select_n | solution.py:331
  89.7 0.7 copy-done.16
  90.4 17.2 %carried.1 = (bf16[128,2048]{1,0:T(8,128)(2,1)}, bf16[128,256]{1,0:T(8,128)(2,1)}, bf16[128,256]{1,0:T(8,128)(2,1)}, f32[32,128]{1,0:T(8,128)}, bf16[128,2048]{1...) custom-call(s32[1]{0:T(128)S(6)} %copy.40.len_ref, ...), custom_call_target="tpu_custom_call" | custom-call | tf_op jit(solution)/shard_map/carried/pallas_call | solution.py:430
  107.7 0.7 fusion.1.x_ref
  108.3 12.1 %shard_map.243 = f32[4,16,2560]{2,1,0:T(8,128)} custom-call(f32[16,2560]{1,0:T(8,128)} %fusion.1.x_ref), custom_call_target="tpu_custom_call" | custom-call | tf_op jit(solution)/shard_map/pallas_call | solution.py:298
  120.4 1.0 slice_reduce_fusion
  121.4 0.9 bitcast_select_fusion
  122.4 1.3 %scatter.14 = bf16[128,256]{1,0:T(8,128)(2,1)} dynamic-update-slice(bf16[128,256]{1,0:T(8,128)(2,1)} %get-tuple-element.95, bf16[3,256]{1,0:T(4,128)(2,1)S(1)} %get-tuple-element.114, s32[]{:T(128)} %constant.96.clone.1, s32[]{:T(128)} %constant.88.clone.1) | dynamic-update-slice | bytes 3076 | tf_op jit(solution)/shard_map/scatter | solution.py:451
  123.7 1.3 %scatter.11 = bf16[128,256]{1,0:T(8,128)(2,1)} dynamic-update-slice(bf16[128,256]{1,0:T(8,128)(2,1)} %get-tuple-element.93, bf16[3,256]{1,0:T(4,128)(2,1)S(1)} %get-tuple-element.115, s32[]{:T(128)} %constant.96.clone.1, s32[]{:T(128)} %constant.88.clone.1) | dynamic-update-slice | bytes 3076 | tf_op jit(solution)/shard_map/scatter | solution.py:451
  125.0 1.4 %scatter.10 = bf16[128,2048]{1,0:T(8,128)(2,1)} dynamic-update-slice(bf16[128,2048]{1,0:T(8,128)(2,1)} %get-tuple-element.85, bf16[3,2048]{1,0:T(4,128)(2,1)S(1)} %fusion.4, s32[]{:T(128)} %constant.96.clone.1, s32[]{:T(128)} %constant.88.clone.1) | dynamic-update-slice | bytes 24580 | tf_op jit(solution)/shard_map/scatter | solution.py:451
  (82 shorter events, 1.6 us)
Async XLA Ops:
  0.6 0.8 slice-start
  0.7 14.5 %copy-start.12 = (bf16[1,128,256]{2,1,0:T(8,128)(2,1)S(1)}, bf16[1,128,256]{2,1,0:T(8,128)(2,1)}, u32[]{:S(2)}) copy-start(bf16[1,128,256]{2,1,0:T(8,128)(2,1)} %param.32) | copy-start | bytes 196612
  0.7 0.8 slice-start.1
  1.5 13.6 %copy-start.10 = (bf16[128,256]{1,0:T(8,128)(2,1)S(1)}, bf16[128,256]{1,0:T(8,128)(2,1)}, u32[]{:S(2)}) copy-start(bf16[128,256]{1,0:T(8,128)(2,1)} %pc.5) | copy-start | bytes 196612
  1.5 13.7 %copy-start.11 = (bf16[1,128,256]{2,1,0:T(8,128)(2,1)S(1)}, bf16[1,128,256]{2,1,0:T(8,128)(2,1)}, u32[]{:S(2)}) copy-start(bf16[1,128,256]{2,1,0:T(8,128)(2,1)} %param.31) | copy-start | bytes 196612
  2.1 13.0 %copy-start = (bf16[128,2048]{1,0:T(8,128)(2,1)S(1)}, bf16[128,2048]{1,0:T(8,128)(2,1)}, u32[]{:S(2)}) copy-start(bf16[128,2048]{1,0:T(8,128)(2,1)} %px.5) | copy-start | bytes 1572868
  2.1 13.0 %copy-start.1 = (bf16[128,2048]{1,0:T(8,128)(2,1)S(1)}, bf16[128,2048]{1,0:T(8,128)(2,1)}, u32[]{:S(2)}) copy-start(bf16[128,2048]{1,0:T(8,128)(2,1)} %pg.5) | copy-start | bytes 1572868
  12.9 0.8 copy-start.32
  12.9 2.3 %copy-start.9 = (bf16[128,256]{1,0:T(8,128)(2,1)S(1)}, bf16[128,256]{1,0:T(8,128)(2,1)}, u32[]{:S(2)}) copy-start(bf16[128,256]{1,0:T(8,128)(2,1)} %pb.5) | copy-start | bytes 196612
  13.7 1.5 %copy-start.13 = (f32[32,128]{1,0:T(8,128)S(1)}, f32[32,128]{1,0:T(8,128)}, u32[]{:S(2)}) copy-start(f32[32,128]{1,0:T(8,128)} %pdt.5) | copy-start | bytes 49156
  15.8 1.0 copy-start.2
  16.8 1.0 copy-start.4
  25.7 7.5 %copy-start.8 = (f32[128,2048]{1,0:T(8,128)}, f32[128,2048]{1,0:T(8,128)S(1)}, u32[]{:S(2)}) copy-start(f32[128,2048]{1,0:T(8,128)S(1)} %get-tuple-element.75) | copy-start | bytes 3145732
  25.7 7.5 %collective-permute-start.1 = (f32[128,2048]{1,0:T(8,128)S(1)}, f32[128,2048]{1,0:T(8,128)}, u32[]{:S(2)}, u32[]{:S(2)}) collective-permute-start(f32[128,2048]{1,0:T(8,128)S(1)} %get-tuple-element.74), channel_id=1, source_target_pairs={{0,4},{4,0},{8,12},{12,8},{1,5},{5,1},{9,13},{13,9},{2,6},{6,2},{1... | collective-permute-start | bytes 3145736 | tf_op jit(solution)/shard_map/ppermute | solution.py:314
  25.7 7.5 %collective-permute-start.3 = (f32[128,2048]{1,0:T(8,128)S(1)}, f32[128,2048]{1,0:T(8,128)}, u32[]{:S(2)}, u32[]{:S(2)}) collective-permute-start(f32[128,2048]{1,0:T(8,128)S(1)} %get-tuple-element.75), channel_id=1, source_target_pairs={{0,4},{4,0},{8,12},{12,8},{1,5},{5,1},{9,13},{13,9},{2,6},{6,2},{1... | collective-permute-start | bytes 3145736 | tf_op jit(solution)/shard_map/ppermute | solution.py:314
  26.2 7.0 %collective-permute-start.4 = (f32[128,2048]{1,0:T(8,128)}, f32[128,2048]{1,0:T(8,128)}, u32[]{:S(2)}, u32[]{:S(2)}) collective-permute-start(f32[128,2048]{1,0:T(8,128)} %get-tuple-element.76), channel_id=1, source_target_pairs={{0,4},{4,0},{8,12},{12,8},{1,5},{5,1},{9,13},{13,9},{2,6},{6,2},{1... | collective-permute-start | bytes 3145736 | tf_op jit(solution)/shard_map/ppermute | solution.py:314
  26.9 4.8 %collective-permute-start = (f32[1,2048]{1,0:T(1,128)}, f32[1,2048]{1,0:T(1,128)}, u32[]{:S(2)}, u32[]{:S(2)}) collective-permute-start(f32[1,2048]{1,0:T(1,128)} %slice.129), channel_id=1, source_target_pairs={{0,4},{4,0},{8,12},{12,8},{1,5},{5,1},{9,13},{13,9},{2,6},{6,2},{1... | collective-permute-start | bytes 24584 | tf_op jit(solution)/shard_map/ppermute | solution.py:314
  33.2 7.6 %copy-start.3 = (bf16[1,128,2048]{2,1,0:T(8,128)(2,1)S(1)}, bf16[1,128,2048]{2,1,0:T(8,128)(2,1)}, u32[]{:S(2)}) copy-start(bf16[1,128,2048]{2,1,0:T(8,128)(2,1)} %param.30) | copy-start | bytes 1572868
  33.2 7.6 %copy-start.5 = (bf16[1,128,2048]{2,1,0:T(8,128)(2,1)S(1)}, bf16[1,128,2048]{2,1,0:T(8,128)(2,1)}, u32[]{:S(2)}) copy-start(bf16[1,128,2048]{2,1,0:T(8,128)(2,1)} %param.34) | copy-start | bytes 1572868
  33.2 7.6 %copy-start.15 = (f32[32,1,128]{2,1,0:T(1,128)S(1)}, f32[32,1,128]{2,1,0:T(1,128)}, u32[]{:S(2)}) copy-start(f32[32,1,128]{2,1,0:T(1,128)} %param.33) | copy-start | bytes 49156
  33.2 7.6 %copy-start.18 = (bf16[4,2048]{1,0:T(4,128)(2,1)S(1)}, bf16[4,2048]{1,0:T(4,128)(2,1)}, u32[]{:S(2)}) copy-start(bf16[4,2048]{1,0:T(4,128)(2,1)} %tx.5) | copy-start | bytes 49156
  33.2 7.6 %copy-start.23 = (bf16[4,256]{1,0:T(4,128)(2,1)S(1)}, bf16[4,256]{1,0:T(4,128)(2,1)}, u32[]{:S(2)}) copy-start(bf16[4,256]{1,0:T(4,128)(2,1)} %tc.5) | copy-start | bytes 6148
  37.9 2.9 %copy-start.21 = (bf16[4,256]{1,0:T(4,128)(2,1)S(1)}, bf16[4,256]{1,0:T(4,128)(2,1)}, u32[]{:S(2)}) copy-start(bf16[4,256]{1,0:T(4,128)(2,1)} %tb.5) | copy-start | bytes 6148
  37.9 2.9 %copy-start.27 = (s32[1,128]{1,0:T(1,128)S(1)}, s32[1,128]{1,0:T(1,128)}, u32[]{:S(2)}) copy-start(s32[1,128]{1,0:T(1,128)} %mask_ref.5) | copy-start | bytes 1540
  37.9 47.6 %collective-permute-start.2 = (f32[128,2048]{1,0:T(8,128)}, f32[128,2048]{1,0:T(8,128)}, u32[]{:S(2)}, u32[]{:S(2)}) collective-permute-start(f32[128,2048]{1,0:T(8,128)} %get-tuple-element.120), channel_id=1, source_target_pairs={{0,8},{4,12},{8,0},{12,4},{1,9},{5,13},{9,1},{13,5},{2,10},{6,14},... | collective-permute-start | bytes 3145736 | tf_op jit(solution)/shard_map/ppermute | solution.py:314
  39.3 46.2 %collective-permute-start.5 = (f32[128,2048]{1,0:T(8,128)}, f32[128,2048]{1,0:T(8,128)}, u32[]{:S(2)}, u32[]{:S(2)}) collective-permute-start(f32[128,2048]{1,0:T(8,128)} %get-tuple-element.110), channel_id=1, source_target_pairs={{0,8},{4,12},{8,0},{12,4},{1,9},{5,13},{9,1},{13,5},{2,10},{6,14},... | collective-permute-start | bytes 3145736 | tf_op jit(solution)/shard_map/ppermute | solution.py:314
  39.4 46.1 %collective-permute-start.6 = (f32[1,2048]{1,0:T(1,128)}, f32[1,2048]{1,0:T(1,128)S(1)}, u32[]{:S(2)}, u32[]{:S(2)}) collective-permute-start(f32[1,2048]{1,0:T(1,128)} %get-tuple-element.123), channel_id=1, source_target_pairs={{0,8},{4,12},{8,0},{12,4},{1,9},{5,13},{9,1},{13,5},{2,10},{6,14},... | collective-permute-start | bytes 24584 | tf_op jit(solution)/shard_map/ppermute | solution.py:314
  40.8 44.7 %copy-start.29 = (f32[1,2048]{1,0:T(1,128)S(1)}, f32[1,2048]{1,0:T(1,128)}, u32[]{:S(2)}) copy-start(f32[1,2048]{1,0:T(1,128)} %get-tuple-element.124) | copy-start | bytes 24580
  48.5 1.0 copy-start.6
  49.5 1.0 copy-start.7
  50.5 35.0 %copy-start.28 = (f32[1,2048]{1,0:T(1,128)S(1)}, f32[1,2048]{1,0:T(1,128)}, u32[]{:S(2)}) copy-start(f32[1,2048]{1,0:T(1,128)} %get-tuple-element.122) | copy-start | bytes 24580
  85.5 4.2 %copy-start.19 = (bf16[4,2048]{1,0:T(4,128)(2,1)S(1)}, bf16[4,2048]{1,0:T(4,128)(2,1)}, u32[]{:S(2)}) copy-start(bf16[4,2048]{1,0:T(4,128)(2,1)} %tx.5) | copy-start | bytes 49156
  (11 other events, 7.8 us)
where the time goes:
time: 127 us; the launch traced here: 126 us
  Pallas kernels  52.3 us (41%)
  waiting for transfers between devices  39.4 us (31%)
  other arithmetic  14.4 us (11%)
  local copies, waits for them, and re-layouts  14.2 us (11%)
  starting transfers between devices  3.82 us (3%)
  between operations  2.32 us (2%)
    ppermute x7, waiting for transfers between devices, exchange(): return [lax.ppermute(part, 'suf', route) for part in parts]  39.4 us
    pallas_call x2, Pallas kernels, gather_small(): pl.pallas_call(functools.partial(gather_kernel, ways), out_shape=jax.Shap...  21 us
    pallas_call x1, Pallas kernels, shards(): pl.pallas_call(carried_kernel, grid=(groups,), in_specs=base_specs + [sx,...  17.2 us
    pallas_call x1, Pallas kernels, shards(): pl.pallas_call(within_kernel, grid=(groups,), in_specs=base_specs, out_sp...  7.66 us
    unnamed x66, local copies, waits for them, and re-layouts  7.56 us
    pallas_call x1, Pallas kernels, shards(): pl.pallas_call(states_kernel, grid=(groups,), in_specs=base_specs, out_sp...  6.35 us
    select_n x1, other arithmetic, combine(): second = jnp.where(upper, adj + dec * suf, suf)  4.69 us
    select_n x1, other arithmetic, combine(): end = jnp.where(upper, dec * own_ + own, dec_ * own + own_)  4.14 us
  transfers between devices with their start and end apart: 7, of which 2 were waited for; matrix products, arithmetic and copies ran while one was open for 2% of the time, Pallas kernels for 6%

commit v1 on v0

--- a/solution.py
+++ b/solution.py
@@ -38,7 +38,7 @@
 
 
 def conv_pre(halo, u, taps):
-    w = jnp.concatenate([halo.astype(F32), u.astype(F32)], axis=0)
+    w = jnp.concatenate([halo.astype(F32)[8:], u.astype(F32)], axis=0)
     taps = taps.astype(F32)
     out = w[5 : 5 + Q] * taps[0:1]
     for k in range(1, KW):
@@ -90,7 +90,11 @@
 
 
 def widen(rows, spread):
-    return lax.dot_general(rows.T, spread, NN, precision=EXACT, preferred_element_type=F32)
+    v = rows.T
+    hi, rest = split(v)
+    lo = (v - hi.astype(F32) - rest.astype(F32)).astype(BF16)
+    e = spread.astype(BF16)
+    return mm(jnp.concatenate([hi, rest, lo], axis=1), jnp.concatenate([e, e, e], axis=0))
 
 
 def row_weight(len_ref, adv_ref, mask_ref):
@@ -185,64 +189,85 @@
     within(sx, sb, sc, sdt, sg, shx, shb, shc, tx, tb, tc, rate, bias, weight, s_dx, s_db, s_dc, s_r)
 
 
-def per_head(spread, value):
+def per_head(value, gather):
     hi, lo = split(value)
-    e = spread.astype(BF16)
-    return mm(e, hi, NT) + mm(e, lo, NT)
+    return mm(jnp.concatenate([hi, lo], axis=1), gather)
 
 
 def carried(x_ref, b_ref, c_ref, dt_ref, g_ref, hx, hb, hc, tx, tb, tc, rate, bias, skip, weight,
-            start, adjoint, in_dx, in_db, in_dc, in_r, dx, db, dc, ddt, lx, lb, lc, tails):
+            state, in_dx, in_db, in_dc, in_r, dx, db, dc, ddt, lefts, tails):
     heads = dt_ref.shape[0]
     spread = expander(heads)
     raw, step, cum = decays(dt_ref, bias, rate)
     pull = jnp.exp(cum)
     if weight is not None:
         pull = pull * weight
-    pull_wide = widen(pull, spread)
     gain = skip[...] if weight is None else skip[...] * weight
-    gain_wide = widen(jnp.broadcast_to(gain, (heads, Q)), spread)
+    gain = jnp.broadcast_to(gain, (heads, Q))
+    last = cum[:, Q - 1 : Q]
+    push = jnp.exp(last - cum) * step
     b_pre = conv_pre(hb[...], b_ref[...], tb[...])
     c_pre = conv_pre(hc[...], c_ref[...], tc[...])
-    x_pre = conv_pre(hx[...], x_ref[...], tx[...])
-    x_act = silu(x_pre)
-    grad = g_ref[...].astype(F32)
+    b_act = split(silu(b_pre))
     c_act = split(silu(c_pre))
-    s_split = split(start[...])
-    pulled = grad * pull_wide
-    across = per_head(spread, pulled * mm3(c_act, s_split))
-    dc_act = in_dc[...] + mm3(split(pulled), s_split, NT)
+    dc_act = in_dc[...]
     db_act = in_db[...]
-    dx_in = in_dx[...]
-    col_sum = per_head(spread, x_act * dx_in)
-    end = jnp.zeros((heads, 1), F32)
-    if adjoint is not None:
-        last = cum[:, Q - 1 : Q]
-        push = widen(jnp.exp(last - cum) * step, spread)
-        b_act = split(silu(b_pre))
-        a_split = split(adjoint[...])
-        moved = push * mm3(b_act, a_split)
-        dx_in = dx_in + moved
-        v = per_head(spread, x_act * moved)
-        col_sum = col_sum + v
-        db_act = db_act + mm3(split(x_act * push), a_split, NT)
-        both = jnp.sum(per_head(spread, start[...] * adjoint[...]), axis=1, keepdims=True)
-        end = jnp.sum(v, axis=1, keepdims=True) + jnp.exp(last) * both
-    change = in_r[...] + across - col_sum
+    width = heads * HD
+    chunk = min(width, 256)
+    across = jnp.zeros((Q, heads), F32)
+    col_sum = jnp.zeros((Q, heads), F32)
+    v = jnp.zeros((Q, heads), F32)
+    both = jnp.zeros((8, heads), F32)
+    first = 0 if weight is None else 3
+    head_of = lax.broadcasted_iota(jnp.int32, (chunk, heads), 1) * HD
+    lane_of = lax.broadcasted_iota(jnp.int32, (chunk, heads), 0)
+
+    def finish(dact, pre, taps, out, left, tail, cols):
+        du, dleft = conv_back(dact, pre, taps)
+        out[:, cols] = du.astype(BF16)
+        left[first : first + 3, cols] = dleft[:3]
+        if tail is not None:
+            tail[:, cols] = du[Q - 8 :]
+
+    for at in range(0, width, chunk):
+        cols = slice(at, at + chunk)
+        inside = (lane_of + at >= head_of) & (lane_of + at < head_of + HD)
+        gather = inside.astype(BF16)
+        gather = jnp.concatenate([gather, gather], axis=0)
+        part = spread[:, cols]
+        grad = g_ref[:, cols].astype(F32)
+        x_pre = conv_pre(hx[:, cols], x_ref[:, cols], tx[:, cols])
+        x_act = silu(x_pre)
+        start, adjoint = state(cols)
+        s_split = split(start)
+        pulled = grad * widen(pull, part)
+        across = across + per_head(pulled * mm3(c_act, s_split), gather)
+        dc_act = dc_act + mm3(split(pulled), s_split, NT)
+        dx_in = in_dx[:, cols]
+        if adjoint is not None:
+            push_wide = widen(push, part)
+            a_split = split(adjoint)
+            moved = push_wide * mm3(b_act, a_split)
+            dx_in = dx_in + moved
+            v = v + per_head(x_act * moved, gather)
+            db_act = db_act + mm3(split(x_act * push_wide), a_split, NT)
+            product = jnp.sum(start * adjoint, axis=0, keepdims=True)
+            both = both + per_head(jnp.broadcast_to(product, (8, chunk)), gather)
+        col_sum = col_sum + per_head(x_act * dx_in, gather)
+        dx_act = dx_in + widen(gain, part) * grad
+        finish(dx_act, x_pre, tx[:, cols], dx, lefts[0], tails and tails[0], cols)
+    whole = slice(0, N)
+    finish(db_act, b_pre, tb[...], db, lefts[1], tails and tails[1], whole)
+    finish(dc_act, c_pre, tc[...], dc, lefts[2], tails and tails[2], whole)
+    end = jnp.sum(v, axis=0, keepdims=True).T
+    if weight is None:
+        end = end + jnp.exp(last) * both.T[:, :1]
+    cols_t = col_sum.T
+    change = in_r[...] + across.T - cols_t
     dlog = end + lax.dot_general(
         change, tri(True).astype(F32), NN, precision=EXACT, preferred_element_type=F32
     )
-    ddt[...] = (col_sum / step - rate[...] * dlog) * jax.nn.sigmoid(raw)
-    for dact, pre, taps, out, left, tail in (
-        (dx_in + gain_wide * grad, x_pre, tx, dx, lx, 0),
-        (db_act, b_pre, tb, db, lb, 1),
-        (dc_act, c_pre, tc, dc, lc, 2),
-    ):
-        du, dleft = conv_back(dact, pre, taps[...])
-        out[...] = du.astype(BF16)
-        left[...] = dleft
-        if tails is not None:
-            tails[tail][...] = du[Q - 8 :]
+    ddt[...] = (cols_t / step - rate[...] * dlog) * jax.nn.sigmoid(raw)
 
 
 def carried_kernel(
@@ -250,68 +275,185 @@
     px, pb, pc, pdt, pg, phx, phb, phc,
     sx, sb, sc, sdt, sg, shx, shb, shc,
     tx, tb, tc, rate, bias, skip,
-    p_start, p_adj, s_start,
+    start, own, tail, suf, own_q, sec_q, rows,
     p_idx, p_idb, p_idc, p_r, s_idx, s_idb, s_idc, s_r,
     p_dx, p_db, p_dc, p_ddt, s_dx, s_db, s_dc, s_ddt,
-    plx, plb, plc, slx, slb, slc, ptx, ptb, ptc,
+    lx, lb, lc, ptx, ptb, ptc,
 ):
+    for left in (lx, lb, lc):
+        left[...] = jnp.zeros_like(left)
+
+    def prompt_state(cols):
+        other = own_q[:, cols].astype(F32)
+        second = sec_q[:, cols].astype(F32)
+        begin = start[:, cols] + rows[0:1, cols] * other
+        adjoint = tail[:, cols] + rows[3:4, cols] * second + rows[4:5, cols] * suf[:, cols]
+        return begin, adjoint
+
+    def suffix_state(cols):
+        other = own_q[:, cols].astype(F32)
+        return rows[1:2, cols] * own[:, cols] + rows[2:3, cols] * other, None
+
     carried(px, pb, pc, pdt, pg, phx, phb, phc, tx, tb, tc, rate, bias, skip, None,
-            p_start, p_adj, p_idx, p_idb, p_idc, p_r, p_dx, p_db, p_dc, p_ddt,
-            plx, plb, plc, (ptx, ptb, ptc))
+            prompt_state, p_idx, p_idb, p_idc, p_r, p_dx, p_db, p_dc, p_ddt,
+            (lx, lb, lc), (ptx, ptb, ptc))
     weight = row_weight(len_ref, adv_ref, mask_ref)
     carried(sx, sb, sc, sdt, sg, shx, shb, shc, tx, tb, tc, rate, bias, skip, weight,
-            s_start, None, s_idx, s_idb, s_idc, s_r, s_dx, s_db, s_dc, s_ddt,
-            slx, slb, slc, None)
-
-
-def gather_kernel(ways, x_ref, out_ref, send, recv, own):
-    me = lax.axis_index("suf")
+            suffix_state, s_idx, s_idb, s_idc, s_r, s_dx, s_db, s_dc, s_ddt,
+            (lx, lb, lc), None)
+
+
+def remote(src, dst, send, recv, target):
+    return pltpu.make_async_remote_copy(
+        src_ref=src,
+        dst_ref=dst,
+        send_sem=send,
+        recv_sem=recv,
+        device_id={"suf": target},
+        device_id_type=MESH,
+    )
+
+
+def greet(ways, me):
     barrier = pltpu.get_barrier_semaphore()
     for d in range(1, ways):
         pl.semaphore_signal(
             barrier, inc=1, device_id={"suf": lax.rem(me + d, ways)}, device_id_type=MESH
         )
     pl.semaphore_wait(barrier, ways - 1)
-    copies = []
-    for d in range(1, ways):
-        copies.append(
-            pltpu.make_async_remote_copy(
-                src_ref=x_ref,
-                dst_ref=out_ref.at[d],
-                send_sem=send.at[d],
-                recv_sem=recv.at[d],
-                device_id={"suf": lax.rem(me + d, ways)},
-                device_id_type=MESH,
-            )
-        )
-        copies[-1].start()
-    mine = pltpu.make_async_copy(x_ref, out_ref.at[0], own)
-    mine.start()
-    mine.wait()
-    for copy in copies:
-        copy.wait()
-
-
-def gather_small(block, ways, ident):
-    if ways == 1:
-        return block[None]
+
+
+def halo_kernel(ways, x_ref, out_ref, send, recv):
+    me = lax.axis_index("suf")
+    last = ways - 1
+    greet(ways, me)
+    right = remote(x_ref, out_ref.at[0], send.at[last], recv.at[0], lax.rem(me + 1, ways))
+    spread = [remote(x_ref, out_ref.at[1], send.at[i], recv.at[1], i) for i in range(last)]
+
+    @pl.when(me < last)
+    def _():
+        right.start()
+
+    @pl.when(me == last)
+    def _():
+        for copy in spread:
+            copy.start()
+        out_ref[1] = x_ref[...]
+        for copy in spread:
+            copy.wait_send()
+
+    @pl.when(me == 0)
+    def _():
+        out_ref[0] = jnp.zeros_like(x_ref)
+
+    @pl.when(me < last)
+    def _():
+        right.wait_send()
+        spread[0].wait_recv()
+
+    @pl.when(me > 0)
+    def _():
+        right.wait_recv()
+
+
+def halo(block, ways):
     return pl.pallas_call(
-        functools.partial(gather_kernel, ways),
-        out_shape=jax.ShapeDtypeStruct((ways,) + block.shape, block.dtype),
+        functools.partial(halo_kernel, ways),
+        out_shape=jax.ShapeDtypeStruct((2,) + block.shape, block.dtype),
+        in_specs=[pl.BlockSpec(memory_space=pltpu.VMEM)],
+        out_specs=pl.BlockSpec(memory_space=pltpu.VMEM),
+        scratch_shapes=[pltpu.SemaphoreType.DMA((ways,)), pltpu.SemaphoreType.DMA((2,))],
+        compiler_params=pltpu.CompilerParams(collective_id=0, has_side_effects=True),
+        name="halo",
+    )(block)
+
+
+def sum_kernel(ways, x_ref, out_ref, slots, send, recv):
+    me = lax.axis_index("suf")
+    last = ways - 1
+    greet(ways, me)
+    left = remote(x_ref, slots.at[last], send.at[0], recv.at[last], lax.rem(me + last, ways))
+    up = remote(x_ref, slots.at[me], send.at[1], recv.at[me], last)
+
+    @pl.when(me > 0)
+    def _():
+        left.start()
+
+    @pl.when(me < last)
+    def _():
+        up.start()
+
+    @pl.when(me > 0)
+    def _():
+        left.wait_send()
+
+    @pl.when(me < last)
+    def _():
+        up.wait_send()
+        left.wait_recv()
+        out_ref[0:3] = slots[last][0:3]
+
+    @pl.when(me == last)
+    def _():
+        total = x_ref[3:6]
+        for i in range(last):
+            remote(x_ref, slots.at[i], send.at[1], recv.at[i], 0).wait_recv()
+            total = total + slots[i][3:6]
+        out_ref[0:3] = total
+
+
+def sum_rows(block, ways):
+    return pl.pallas_call(
+        functools.partial(sum_kernel, ways),
+        out_shape=jax.ShapeDtypeStruct(block.shape, block.dtype),
         in_specs=[pl.BlockSpec(memory_space=pltpu.VMEM)],
         out_specs=pl.BlockSpec(memory_space=pltpu.VMEM),
         scratch_shapes=[
+            pltpu.VMEM((ways,) + block.shape, block.dtype),
+            pltpu.SemaphoreType.DMA((2,)),
             pltpu.SemaphoreType.DMA((ways,)),
-            pltpu.SemaphoreType.DMA((ways,)),
-            pltpu.SemaphoreType.DMA,
         ],
-        compiler_params=pltpu.CompilerParams(collective_id=ident, has_side_effects=True),
+        compiler_params=pltpu.CompilerParams(collective_id=1, has_side_effects=True),
+        name="sum_rows",
     )(block)
+
+
+def fix_kernel(extra, tx, tb, tc, dx, db, dc, ox, ob, oc):
+    at = 0
+    row = lax.broadcasted_iota(jnp.int32, (8, 1), 0)
+    for tail, source, out in ((tx, dx, ox), (tb, db, ob), (tc, dc, oc)):
+        width = tail.shape[1]
+        rows = extra[:, at : at + width]
+        moved = jnp.concatenate([jnp.zeros((5, width), F32), rows[0:3]], axis=0)
+        fixed = tail[...] + jnp.where(row >= 5, moved, 0.0)
+        out[...] = jnp.concatenate([source[...].astype(F32)[:8], fixed], axis=0).astype(BF16)
+        at += width
+
+
+def fix(extra, tails, grads):
+    full_specs = [pl.BlockSpec(memory_space=pltpu.VMEM)] * 4
+    ends = [pl.BlockSpec((16, g.shape[1]), lambda i: (Q // 16 - 1, 0)) for g in grads]
+    return pl.pallas_call(
+        fix_kernel,
+        grid=(1,),
+        in_specs=full_specs + ends,
+        out_specs=ends,
+        out_shape=[jax.ShapeDtypeStruct(g.shape, g.dtype) for g in grads],
+        input_output_aliases={4: 0, 5: 1, 6: 2},
+        name="fix",
+    )(extra, *tails, *grads)
 
 
 def exchange(parts, bit, ways):
     route = [(i, i ^ bit) for i in range(ways)]
     return [lax.ppermute(part, "suf", route) for part in parts]
+
+
+def code(value):
+    top = jnp.max(jnp.abs(value), axis=0, keepdims=True)
+    safe = top > 1e-30
+    inverse = jnp.where(safe, 32767.0 / jnp.where(safe, top, 1.0), 0.0)
+    return jnp.round(value * inverse).astype(jnp.int16), top * (1.0 / 32767.0)
 
 
 def combine(own, adj, suf, dec, ways):
@@ -321,19 +463,8 @@
     tail = jnp.zeros_like(adj)
     after = jnp.ones_like(dec)
     bit = 1
-    while bit < ways:
+    while bit * 2 < ways:
         upper = (me & bit) != 0
-        final = bit * 2 == ways
-        if final:
-            second = jnp.where(upper, adj + dec * suf, suf)
-            own_, second_, dec_ = exchange((own, second, dec), bit, ways)
-            start = jnp.where(upper, before * own_ + start, start)
-            end = jnp.where(upper, dec * own_ + own, dec_ * own + own_)
-            total = suf + second_
-            tail = jnp.where(
-                upper, tail + after * total, tail + after * (second_ + dec_ * suf)
-            )
-            return start, end, tail
         own_, adj_, suf_, dec_ = exchange((own, adj, suf, dec), bit, ways)
         start = jnp.where(upper, before * own_ + start, start)
         before = jnp.where(upper, before * dec_, before)
@@ -344,7 +475,34 @@
         suf = suf + suf_
         dec = dec * dec_
         bit *= 2
-    return start, own, tail + after * suf
+    upper = (me & bit) != 0
+    core = me & 1
+    half = own.shape[1] // 2
+
+    def mine(value):
+        return jnp.where(core == 0, value[:, :half], value[:, half:])
+
+    second = jnp.where(upper, adj + dec * suf, suf)
+    own_q, own_s = code(mine(own))
+    sec_q, sec_s = code(mine(second))
+    got = exchange((own_q, sec_q, jnp.concatenate([own_s, sec_s, mine(dec)], axis=0)), bit, ways)
+    other = exchange(got, 1, ways)
+
+    def whole(a, b):
+        return jnp.where(core == 0, jnp.concatenate([a, b], 1), jnp.concatenate([b, a], 1))
+
+    own_q, sec_q, small = [whole(a, b) for a, b in zip(got, other)]
+    own_s, sec_s, dec_ = small[0:1], small[1:2], small[2:3]
+    zero = jnp.zeros_like(dec)
+    rows = [
+        jnp.where(upper, before, zero) * own_s,
+        jnp.where(upper, jnp.ones_like(dec), dec_),
+        jnp.where(upper, dec, jnp.ones_like(dec)) * own_s,
+        after * sec_s,
+        jnp.where(upper, after, after * dec_),
+        zero, zero, zero,
+    ]
+    return start, own, tail, suf, own_q, sec_q, jnp.concatenate(rows, axis=0)
 
 
 def shards(
@@ -353,22 +511,21 @@
     lengths, loss_mask, advantage, conv_x, conv_b, conv_c, decay_rate, dt_bias, skip,
 ):
     ways = lax.axis_size("suf")
-    me = lax.axis_index("suf")
     heads = decay_rate.shape[0]
     groups = conv_b.shape[1] // N
     per = heads // groups
     wide = per * HD
     full = heads * HD
     nb = groups * N
-    margin = KW - 1
 
     tails = jnp.concatenate([prefix_x[-16:], prefix_b[-16:], prefix_c[-16:]], axis=1)
-    gathered = gather_small(tails, ways, 0)[:, 8:]
-    left = jnp.where(me == 0, jnp.zeros_like(gathered[0]), gathered[1 % ways])
-    context = lax.dynamic_index_in_dim(gathered, lax.rem(me + 1, ways), 0, False)
-
-    def cut(block):
-        return block[:, :full], block[:, full : full + nb], block[:, full + nb :]
+    halos = halo(tails, ways)
+
+    def halo_specs(slot):
+        def at(width, first):
+            return pl.BlockSpec((None, 16, width), lambda g: (slot, 0, first // width + g))
+
+        return [at(wide, 0), at(N, full), at(N, full + nb)]
 
     sm = pl.BlockSpec(memory_space=pltpu.SMEM)
     sx = pl.BlockSpec((Q, wide), lambda g: (0, g))
@@ -379,16 +536,16 @@
     kx = pl.BlockSpec((KW, wide), lambda g: (0, g))
     kb = pl.BlockSpec((KW, N), lambda g: (0, g))
     ph = pl.BlockSpec((per, 1), lambda g: (g, 0))
-    half = [sx, sb, sb, sdt, sx, hx, hb, hb]
+    half = [sx, sb, sb, sdt, sx]
     base_specs = (
-        [sm, sm, pl.BlockSpec((1, Q), lambda g: (0, 0))] + half + half + [kx, kb, kb, ph, ph, ph]
+        [sm, sm, pl.BlockSpec((1, Q), lambda g: (0, 0))] + half + halo_specs(0) + half + halo_specs(1) + [kx, kb, kb, ph, ph, ph]
     )
     base = (
         (lengths, advantage, loss_mask)
         + (prefix_x, prefix_b, prefix_c, prefix_dt, prefix_grad)
-        + cut(left)
+        + (halos,) * 3
         + (suffix_x[0], suffix_b[0], suffix_c[0], suffix_dt[:, 0], suffix_grad[0])
-        + cut(context)
+        + (halos,) * 3
         + (conv_x, conv_b, conv_c, decay_rate[:, None], dt_bias[:, None], skip[:, None])
     )
 
@@ -422,33 +579,23 @@
         name="within",
     )(*base)
 
-    start, end, adjoint = combine(own, adj, suf, dec[:1], ways)
-
-    out_specs = [sx, sb, sb, sdt] * 2 + [hx, hb, hb] * 3
+    states = combine(own, adj, suf, dec[:1], ways)
+
+    out_specs = [sx, sb, sb, sdt] * 2 + [hx, hb, hb] * 2
     out_shape = [shape(Q, full, BF16), shape(Q, nb, BF16), shape(Q, nb, BF16), shape(heads, Q)] * 2
-    out_shape += [shape(8, full), shape(8, nb), shape(8, nb)] * 3
+    out_shape += [shape(8, full), shape(8, nb), shape(8, nb)] * 2
     outs = pl.pallas_call(
         carried_kernel,
         grid=(groups,),
-        in_specs=base_specs + [sx, sx, sx] + inner_specs * 2,
+        in_specs=base_specs + [sx] * 6 + [hx] + inner_specs * 2,
         out_specs=out_specs,
         out_shape=out_shape,
         compiler_params=params,
         name="carried",
-    )(*base, start, adjoint, end, *inner)
-
-    lefts = jnp.concatenate(outs[8:11], axis=1)[:margin]
-    sufs = jnp.concatenate(outs[11:14], axis=1)[:margin]
-    pad = jnp.zeros((8 - margin, lefts.shape[1]), F32)
-    message = jnp.concatenate([lefts, pad, sufs, pad], axis=0)
-    got = gather_small(message, ways, 1)
-    extra = jnp.where(
-        me == ways - 1, jnp.sum(got[:, 8 : 8 + margin], axis=0), got[ways - 1, :margin]
-    )
-    finished = []
-    for at, add in enumerate(cut(extra)):
-        tail = (outs[14 + at][-margin:] + add).astype(BF16)
-        finished.append(outs[at].at[-margin:].set(tail))
+    )(*base, *states, *inner)
+
+    extra = sum_rows(jnp.concatenate(outs[8:11], axis=1), ways)
+    finished = fix(extra, outs[11:14], outs[:3])
     return (
         *finished,
         outs[3],

time: 127 us -> 88.3 us (0.70)
  waiting for transfers between devices: 39.4 us -> 4.97 us
  Pallas kernels: 52.3 us -> 43.1 us
  local copies, waits for them, and re-layouts: 14.2 us -> 21.6 us
  other arithmetic: 14.4 us -> 9.87 us
  starting transfers between devices: 3.82 us -> 5.23 us
    ppermute x7 -> x10, waiting for transfers between devices: 39.4 us -> 4.97 us  [exchange(): return [lax.ppermute(part, 'suf', route) for part in parts]]
    pallas_call x3 -> x4, Pallas kernels: 38.3 us -> 29 us  [the longest x1 14.9 us: shards(): pl.pallas_call(carried_kernel, grid=(groups,), in_specs=base_specs + [sx]...]
    unnamed x66 -> x116, local copies, waits for them, and re-layouts: 7.56 us -> 15.8 us
    scatter x3 -> x0, local copies, waits for them, and re-layouts: 4 us -> none  [shards(): finished.append(outs[at].at[-margin:].set(tail))]
    select_n x4 -> x5, other arithmetic: 7.3 us -> 3.47 us  [the longest x3 2.81 us: whole(): jnp.where(core == 0, jnp.concatenate([a, b], 1), jnp.concatenate([b, a], 1))]
    concatenate x0 -> x2, local copies, waits for them, and re-layouts: none -> 2.16 us  [combine(): return (start, own, tail, suf, own_q, sec_q, jnp.concatenate(rows, axis=0))]
    slice x5 -> x1, local copies, waits for them, and re-layouts: 1.54 us -> 0.01 us  [shards(): states = combine(own, adj, suf, dec[:1], ways)]
    ppermute x7 -> x10, starting transfers between devices: 3.82 us -> 5.23 us  [exchange(): return [lax.ppermute(part, 'suf', route) for part in parts]]
  transfers between devices with their start and end apart: 7 -> 10, of which waited for: 2 -> 4; matrix products, arithmetic and copies ran while one was open for 2% -> 5% of each run, Pallas kernels for 6% -> 9%
where the time goes in v1:
time: 88.3 us; the launch traced here: 87.4 us
  Pallas kernels  43.1 us (49%)
  local copies, waits for them, and re-layouts  21.6 us (24%)
  other arithmetic  9.87 us (11%)
  starting transfers between devices  5.23 us (6%)
  waiting for transfers between devices  4.97 us (6%)
  between operations  2.53 us (3%)
    unnamed x116, local copies, waits for them, and re-layouts  15.8 us
    pallas_call x1, Pallas kernels, shards(): pl.pallas_call(carried_kernel, grid=(groups,), in_specs=base_specs + [sx]...  14.9 us
    pallas_call x1, Pallas kernels, shards(): pl.pallas_call(within_kernel, grid=(groups,), in_specs=base_specs, out_sp...  8.03 us
    pallas_call x1, Pallas kernels, halo(): pl.pallas_call(functools.partial(halo_kernel, ways), out_shape=jax.ShapeD...  7.05 us
    pallas_call x1, Pallas kernels, shards(): pl.pallas_call(states_kernel, grid=(groups,), in_specs=base_specs, out_sp...  6.12 us
    pallas_call x1, Pallas kernels, sum_rows(): pl.pallas_call(functools.partial(sum_kernel, ways), out_shape=jax.ShapeDt...  5.45 us
    ppermute x10, starting transfers between devices, exchange(): return [lax.ppermute(part, 'suf', route) for part in parts]  5.23 us
    ppermute x10, waiting for transfers between devices, exchange(): return [lax.ppermute(part, 'suf', route) for part in parts]  4.97 us
  transfers between devices with their start and end apart: 10, of which 4 were waited for; matrix products, arithmetic and copies ran while one was open for 5% of the time, Pallas kernels for 9%

profile of v1, /device:TPU:1, one launch (start us, length us, event | category | flops | bytes accessed | tf_op | source)
XLA Modules:
  0.0 87.4 jit_solution(3319143120585396350)
XLA Ops:
  0.7 0.8 slice.40
  1.4 0.7 slice.41
  2.8 7.1 %halo.1.phx.phb.phc.shx.shb.shc = bf16[2,16,2560]{2,1,0:T(8,128)(2,1)} custom-call(bf16[16,2560]{1,0:T(8,128)(2,1)} %pad_maximum_fusion.x_ref), custom_call_target="tpu_custom_call" | custom-call | tf_op jit(solution)/shard_map/halo/pallas_call | solution.py:360
  9.8 0.7 copy.36.rate
  10.6 0.8 copy.37.bias
  11.3 0.7 copy.38.skip
  13.5 0.9 %copy-done = bf16[2,16,2560]{2,1,0:T(8,128)(2,1)S(1)} copy-done((bf16[2,16,2560]{2,1,0:T(8,128)(2,1)S(1)}, bf16[2,16,2560]{2,1,0:T(8,128)(2,1)}, u32[]{:S(2)}) %copy-start) | copy-done | bytes 163864
  14.4 1.0 %copy-done.3 = bf16[128,2048]{1,0:T(8,128)(2,1)S(1)} copy-done((bf16[128,2048]{1,0:T(8,128)(2,1)S(1)}, bf16[128,2048]{1,0:T(8,128)(2,1)}, u32[]{:S(2)}) %copy-start.3) | copy-done | bytes 524312
  15.4 1.0 %copy-done.5 = bf16[1,128,2048]{2,1,0:T(8,128)(2,1)S(1)} copy-done((bf16[1,128,2048]{2,1,0:T(8,128)(2,1)S(1)}, bf16[1,128,2048]{2,1,0:T(8,128)(2,1)}, u32[]{:S(2)}) %copy-start.5) | copy-done | bytes 524312
  16.5 1.0 %copy-done.7 = bf16[1,128,2048]{2,1,0:T(8,128)(2,1)S(1)} copy-done((bf16[1,128,2048]{2,1,0:T(8,128)(2,1)S(1)}, bf16[1,128,2048]{2,1,0:T(8,128)(2,1)}, u32[]{:S(2)}) %copy-start.7) | copy-done | bytes 524312
  17.5 0.8 copy-done.12
  18.3 0.8 copy-done.14
  19.2 0.8 copy-done.16
  20.0 0.8 copy-done.18
  21.5 6.1 %states.1 = (f32[128,2048]{1,0:T(8,128)S(1)}, f32[128,2048]{1,0:T(8,128)S(1)}, f32[128,2048]{1,0:T(8,128)}, f32[8,2048]{1,0:T(8,128)S(1)}) custom-call(s32[1]{0:T(128)S(6)} %copy.43.len_ref, f32[1]{0:T(128)S(6)} %copy.44.adv_ref, s32[1,128]{1,0:T(1,128)S(1)} %copy-done.52, bf16[128,2048]{1,0:T(8,128)(2,1)S(1)} %copy-done.2, bf16[128,256]{1,0:T(8,128)(2,1)S(1)} %copy-done.12, ...), custom_call_target="tpu_custom_call" | custom-call | tf_op jit(solution)/shard_map/states/pallas_call | solution.py:557
  28.7 1.7 %collective-permute-done.1 = f32[1,2048]{1,0:T(1,128)S(1)} collective-permute-done((f32[1,2048]{1,0:T(1,128)S(1)}, f32[1,2048]{1,0:T(1,128)S(1)}, u32[]{:S(2)}, u32[]{:S(2)}) %collective-permute-start.1) | collective-permute-done | bytes 8224 | tf_op jit(solution)/shard_map/ppermute | solution.py:449
  30.4 3.0 %collective-permute-done.2 = f32[128,2048]{1,0:T(8,128)} collective-permute-done((f32[128,2048]{1,0:T(8,128)S(1)}, f32[128,2048]{1,0:T(8,128)}, u32[]{:S(2)}, u32[]{:S(2)}) %collective-permute-start.2) | collective-permute-done | bytes 1048608 | tf_op jit(solution)/shard_map/ppermute | solution.py:449
  33.7 4.8 %add_select_fusion = (f32[128,2048]{1,0:T(8,128)S(1)}, f32[128,2048]{1,0:T(8,128)}, f32[128,2048]{1,0:T(8,128)}, f32[128,2048]{1,0:T(8,128)S(1)}, f32[128,2048]{1,0:T(8,128)S(1)}) fusion(f32[128,2048]{1,0:T(8,128)} %copy-done.11, f32[128,2048]{1,0:T(8,128)} %collective-permute-done.2, f32[2048]{0:T(1024)S(1)} %bitcast.34, f32[2048]{0:T(1024)S(1)} %bitcast.35, ...), kind=kLoop, calls=%fused_computation | loop fusion | flops 4194304 | bytes 11558914 | tf_op jit(solution)/shard_map/jit(_where)/select_n | solution.py:485
  38.6 0.9 %collective-permute-start.8 = (f32[3,1024]{1,0:T(4,128)S(1)}, f32[3,1024]{1,0:T(4,128)S(1)}, u32[]{:S(2)}, u32[]{:S(2)}) collective-permute-start(f32[3,1024]{1,0:T(4,128)S(1)} %pad_maximum_fusion.2), channel_id=1, source_target_pairs={{0,8},{4,12},{8,0},{12,4},{1,9},{5,13},{9,1},{13,5},{2,10},{6,14},... | collective-permute-start | bytes 36872 | tf_op jit(solution)/shard_map/ppermute | solution.py:449
  39.6 0.7 collective-permute-start.6
  40.5 0.9 %collective-permute-start.4 = (s16[128,1024]{1,0:T(8,128)(2,1)S(1)}, s16[128,1024]{1,0:T(8,128)(2,1)}, u32[]{:S(2)}, u32[]{:S(2)}) collective-permute-start(s16[128,1024]{1,0:T(8,128)(2,1)S(1)} %round-nearest-even_convert_fusion.1), channel_id=1, source_target_pairs={{0,8},{4,12},{8,0},{12,4},{1,9},{5,13},{9,1},{13,5},{2,10},{6,14},... | collective-permute-start | bytes 786440 | tf_op jit(solution)/shard_map/ppermute | solution.py:449
  41.4 1.2 %collective-permute-start.9 = (f32[3,1024]{1,0:T(4,128)S(1)}, f32[3,1024]{1,0:T(4,128)S(1)}, u32[]{:S(2)}, u32[]{:S(2)}) collective-permute-start(f32[3,1024]{1,0:T(4,128)S(1)} %collective-permute-done.8), channel_id=1, source_target_pairs={{0,4},{4,0},{8,12},{12,8},{1,5},{5,1},{9,13},{13,9},{2,6},{6,2},{1... | collective-permute-start | bytes 36872 | tf_op jit(solution)/shard_map/ppermute | solution.py:449
  42.7 8.0 %within.1 = (f32[128,2048]{1,0:T(8,128)S(1)}, f32[128,256]{1,0:T(8,128)S(1)}, f32[128,256]{1,0:T(8,128)S(1)}, f32[32,128]{1,0:T(8,128)S(1)}, f32[128,2048]{1,0:T...) custom-call(s32[1]{0:T(128)S(6)} %copy.43.len_ref, f32[1]{0:T(128)S(6)} %copy.44.adv_ref, ...), custom_call_target="tpu_custom_call" | custom-call | flops 1610612736 | bytes 6291456 | tf_op jit(solution)/shard_map/within/pallas_call | solution.py:569
  50.8 1.0 %copy-done.9 = f32[128,2048]{1,0:T(8,128)} copy-done((f32[128,2048]{1,0:T(8,128)}, f32[128,2048]{1,0:T(8,128)S(1)}, u32[]{:S(2)}) %copy-start.9) | copy-done | bytes 1048600
  51.8 1.0 %copy-done.10 = f32[128,2048]{1,0:T(8,128)} copy-done((f32[128,2048]{1,0:T(8,128)}, f32[128,2048]{1,0:T(8,128)S(1)}, u32[]{:S(2)}) %copy-start.10) | copy-done | bytes 1048600
  54.7 0.7 copy-done.28
  57.8 1.5 %concatenate.42.rows = f32[8,2048]{1,0:T(8,128)} concatenate(f32[1,2048]{1,0:T(1,128)} %get-tuple-element.81, f32[1,2048]{1,0:T(1,128)} %get-tuple-element.82, f32[1,2048]{1,0:T(1,128)} %get-tuple-element.83, f32[1,2048]{1,0:T(1,128)} %get-tuple-element.80, f32[1,2048]{1,0:T(1,128)} %get-tuple-element.79, f32[3,2048]{1,0:T(4,128)} %concatenate.41), dimensions={0} | concatenate | bytes 131072 | tf_op jit(solution)/shard_map/concatenate | solution.py:505
  59.3 1.3 %add_select_fusion.3.sec_q = s16[128,2048]{1,0:T(8,128)(2,1)S(1)} fusion(s16[128,1024]{1,0:T(8,128)(2,1)} %collective-permute-done.7, s16[128,1024]{1,0:T(8,128)(2,1)} %collective-permute-done.6, pred[]{:T(512)S(6)} %eq.2), kind=kLoop, calls=%fused_computation.5 | loop fusion | flops 786432 | bytes 1048577 | tf_op jit(solution)/shard_map/jit(_where)/select_n | solution.py:492
  60.8 1.5 %add_select_fusion.2.own_q = s16[128,2048]{1,0:T(8,128)(2,1)S(1)} fusion(s16[128,1024]{1,0:T(8,128)(2,1)} %collective-permute-done.5, s16[128,1024]{1,0:T(8,128)(2,1)} %collective-permute-done.4, pred[]{:T(512)S(6)} %eq.2), kind=kLoop, calls=%fused_computation.4 | loop fusion | flops 786432 | bytes 1048577 | tf_op jit(solution)/shard_map/jit(_where)/select_n | solution.py:492
  63.0 14.9 %carried.1 = (bf16[128,2048]{1,0:T(8,128)(2,1)}, bf16[128,256]{1,0:T(8,128)(2,1)}, bf16[128,256]{1,0:T(8,128)(2,1)}, f32[32,128]{1,0:T(8,128)}, bf16[128,2048]{1...) custom-call(s32[1]{0:T(128)S(6)} %copy.43.len_ref, ...), custom_call_target="tpu_custom_call" | custom-call | tf_op jit(solution)/shard_map/carried/pallas_call | solution.py:587
  80.3 5.4 %sum_rows.1.extra = f32[8,2560]{1,0:T(8,128)} custom-call(f32[8,2560]{1,0:T(8,128)} %pad_maximum_fusion.1.x_ref), custom_call_target="tpu_custom_call" | custom-call | tf_op jit(solution)/shard_map/sum_rows/pallas_call | solution.py:406
  85.8 1.6 %fix.1 = (bf16[128,2048]{1,0:T(8,128)(2,1)}, bf16[128,256]{1,0:T(8,128)(2,1)}, bf16[128,256]{1,0:T(8,128)(2,1)}) custom-call(f32[8,2560]{1,0:T(8,128)} %sum_rows.1.extra, f32[8,2048]{1,0:T(8,128)} %copy-done.39, f32[8,256]{1,0:T(8,128)} %copy-done.44, f32[8,256]{1,0:T(8,128)} %copy-done.45, ...), custom_call_target="tpu_custom_call", output_to_operand_aliasing={{0}: (4, {}), {1}: (5, {}), {2}: (6, {})} | custom-call | tf_op jit(solution)/shard_map/fix/pallas_call | solution.py:436
  (136 shorter events, 10.6 us)
Async XLA Ops:
  0.6 12.8 %copy-start.2 = (bf16[128,2048]{1,0:T(8,128)(2,1)S(1)}, bf16[128,2048]{1,0:T(8,128)(2,1)}, u32[]{:S(2)}) copy-start(bf16[128,2048]{1,0:T(8,128)(2,1)} %px.5) | copy-start | bytes 1572868
  9.8 3.6 %copy-start.46 = (bf16[4,256]{1,0:T(4,128)(2,1)S(1)}, bf16[4,256]{1,0:T(4,128)(2,1)}, u32[]{:S(2)}) copy-start(bf16[4,256]{1,0:T(4,128)(2,1)} %tb.5) | copy-start | bytes 6148
  9.8 3.6 %copy-start.49 = (bf16[4,256]{1,0:T(4,128)(2,1)S(1)}, bf16[4,256]{1,0:T(4,128)(2,1)}, u32[]{:S(2)}) copy-start(bf16[4,256]{1,0:T(4,128)(2,1)} %tc.5) | copy-start | bytes 6148
  10.6 2.8 %copy-start.33 = (f32[32,1,128]{2,1,0:T(1,128)S(1)}, f32[32,1,128]{2,1,0:T(1,128)}, u32[]{:S(2)}) copy-start(f32[32,1,128]{2,1,0:T(1,128)} %param.27) | copy-start | bytes 49156
  10.6 2.8 %copy-start.36 = (bf16[4,2048]{1,0:T(4,128)(2,1)S(1)}, bf16[4,2048]{1,0:T(4,128)(2,1)}, u32[]{:S(2)}) copy-start(bf16[4,2048]{1,0:T(4,128)(2,1)} %tx.5) | copy-start | bytes 49156
  11.3 2.1 %copy-start.30 = (f32[32,128]{1,0:T(8,128)S(1)}, f32[32,128]{1,0:T(8,128)}, u32[]{:S(2)}) copy-start(f32[32,128]{1,0:T(8,128)} %pdt.5) | copy-start | bytes 49156
  27.6 6.0 %copy-start.11 = (f32[128,2048]{1,0:T(8,128)}, f32[128,2048]{1,0:T(8,128)S(1)}, u32[]{:S(2)}) copy-start(f32[128,2048]{1,0:T(8,128)S(1)} %get-tuple-element.39) | copy-start | bytes 3145732
  27.6 2.8 %collective-permute-start = (f32[128,2048]{1,0:T(8,128)S(1)}, f32[128,2048]{1,0:T(8,128)}, u32[]{:S(2)}, u32[]{:S(2)}) collective-permute-start(f32[128,2048]{1,0:T(8,128)S(1)} %get-tuple-element.37), channel_id=1, source_target_pairs={{0,4},{4,0},{8,12},{12,8},{1,5},{5,1},{9,13},{13,9},{2,6},{6,2},{1... | collective-permute-start | bytes 3145736 | tf_op jit(solution)/shard_map/ppermute | solution.py:449
  27.6 5.8 %collective-permute-start.2 = (f32[128,2048]{1,0:T(8,128)S(1)}, f32[128,2048]{1,0:T(8,128)}, u32[]{:S(2)}, u32[]{:S(2)}) collective-permute-start(f32[128,2048]{1,0:T(8,128)S(1)} %get-tuple-element.39), channel_id=1, source_target_pairs={{0,4},{4,0},{8,12},{12,8},{1,5},{5,1},{9,13},{13,9},{2,6},{6,2},{1... | collective-permute-start | bytes 3145736 | tf_op jit(solution)/shard_map/ppermute | solution.py:449
  28.1 5.5 %collective-permute-start.3 = (f32[128,2048]{1,0:T(8,128)}, f32[128,2048]{1,0:T(8,128)}, u32[]{:S(2)}, u32[]{:S(2)}) collective-permute-start(f32[128,2048]{1,0:T(8,128)} %get-tuple-element.40), channel_id=1, source_target_pairs={{0,4},{4,0},{8,12},{12,8},{1,5},{5,1},{9,13},{13,9},{2,6},{6,2},{1... | collective-permute-start | bytes 3145736 | tf_op jit(solution)/shard_map/ppermute | solution.py:449
  28.2 2.2 %collective-permute-start.1 = (f32[1,2048]{1,0:T(1,128)S(1)}, f32[1,2048]{1,0:T(1,128)S(1)}, u32[]{:S(2)}, u32[]{:S(2)}) collective-permute-start(f32[1,2048]{1,0:T(1,128)S(1)} %slice.42), channel_id=1, source_target_pairs={{0,4},{4,0},{8,12},{12,8},{1,5},{5,1},{9,13},{13,9},{2,6},{6,2},{1... | collective-permute-start | bytes 24584 | tf_op jit(solution)/shard_map/ppermute | solution.py:449
  30.3 3.3 %copy-start.56 = (f32[1,2048]{1,0:T(1,128)}, f32[1,2048]{1,0:T(1,128)S(1)}, u32[]{:S(2)}) copy-start(f32[1,2048]{1,0:T(1,128)S(1)} %collective-permute-done.1) | copy-start | bytes 24580
  38.6 2.8 %collective-permute-start.8 = (f32[3,1024]{1,0:T(4,128)S(1)}, f32[3,1024]{1,0:T(4,128)S(1)}, u32[]{:S(2)}, u32[]{:S(2)}) collective-permute-start(f32[3,1024]{1,0:T(4,128)S(1)} %pad_maximum_fusion.2), channel_id=1, source_target_pairs={{0,8},{4,12},{8,0},{12,4},{1,9},{5,13},{9,1},{13,5},{2,10},{6,14},... | collective-permute-start | bytes 36872 | tf_op jit(solution)/shard_map/ppermute | solution.py:449
  39.5 3.2 %copy-start.8 = (bf16[1,128,2048]{2,1,0:T(8,128)(2,1)S(1)}, bf16[1,128,2048]{2,1,0:T(8,128)(2,1)}, u32[]{:S(2)}) copy-start(bf16[1,128,2048]{2,1,0:T(8,128)(2,1)} %param.28) | copy-start | bytes 1572868
  39.5 3.2 %copy-start.15 = (bf16[128,256]{1,0:T(8,128)(2,1)S(1)}, bf16[128,256]{1,0:T(8,128)(2,1)}, u32[]{:S(2)}) copy-start(bf16[128,256]{1,0:T(8,128)(2,1)} %pc.5) | copy-start | bytes 196612
  39.5 3.2 %copy-start.17 = (bf16[1,128,256]{2,1,0:T(8,128)(2,1)S(1)}, bf16[1,128,256]{2,1,0:T(8,128)(2,1)}, u32[]{:S(2)}) copy-start(bf16[1,128,256]{2,1,0:T(8,128)(2,1)} %param.25) | copy-start | bytes 196612
  39.5 3.2 %copy-start.19 = (bf16[1,128,256]{2,1,0:T(8,128)(2,1)S(1)}, bf16[1,128,256]{2,1,0:T(8,128)(2,1)}, u32[]{:S(2)}) copy-start(bf16[1,128,256]{2,1,0:T(8,128)(2,1)} %param.26) | copy-start | bytes 196612
  39.5 3.2 %copy-start.37 = (bf16[4,2048]{1,0:T(4,128)(2,1)S(1)}, bf16[4,2048]{1,0:T(4,128)(2,1)}, u32[]{:S(2)}) copy-start(bf16[4,2048]{1,0:T(4,128)(2,1)} %tx.5) | copy-start | bytes 49156
  39.6 16.4 %collective-permute-start.6 = (s16[128,1024]{1,0:T(8,128)(2,1)S(1)}, s16[128,1024]{1,0:T(8,128)(2,1)}, u32[]{:S(2)}, u32[]{:S(2)}) collective-permute-start(s16[128,1024]{1,0:T(8,128)(2,1)S(1)} %round-nearest-even_convert_fusion), channel_id=1, source_target_pairs={{0,8},{4,12},{8,0},{12,4},{1,9},{5,13},{9,1},{13,5},{2,10},{6,14},... | collective-permute-start | bytes 786440 | tf_op jit(solution)/shard_map/ppermute | solution.py:449
  40.3 2.3 %copy-start.1 = (bf16[2,16,2560]{2,1,0:T(8,128)(2,1)S(1)}, bf16[2,16,2560]{2,1,0:T(8,128)(2,1)}, u32[]{:S(2)}) copy-start(bf16[2,16,2560]{2,1,0:T(8,128)(2,1)} %halo.1.phx.phb.phc.shx.shb.shc) | copy-start | bytes 491524
  40.3 2.3 %copy-start.4 = (bf16[128,2048]{1,0:T(8,128)(2,1)S(1)}, bf16[128,2048]{1,0:T(8,128)(2,1)}, u32[]{:S(2)}) copy-start(bf16[128,2048]{1,0:T(8,128)(2,1)} %pg.5) | copy-start | bytes 1572868
  40.3 2.3 %copy-start.6 = (bf16[1,128,2048]{2,1,0:T(8,128)(2,1)S(1)}, bf16[1,128,2048]{2,1,0:T(8,128)(2,1)}, u32[]{:S(2)}) copy-start(bf16[1,128,2048]{2,1,0:T(8,128)(2,1)} %param.24) | copy-start | bytes 1572868
  40.3 2.3 %copy-start.13 = (bf16[128,256]{1,0:T(8,128)(2,1)S(1)}, bf16[128,256]{1,0:T(8,128)(2,1)}, u32[]{:S(2)}) copy-start(bf16[128,256]{1,0:T(8,128)(2,1)} %pb.5) | copy-start | bytes 196612
  40.4 2.3 %copy-start.31 = (f32[32,128]{1,0:T(8,128)S(1)}, f32[32,128]{1,0:T(8,128)}, u32[]{:S(2)}) copy-start(f32[32,128]{1,0:T(8,128)} %pdt.5) | copy-start | bytes 49156
  40.4 2.3 %copy-start.34 = (f32[32,1,128]{2,1,0:T(1,128)S(1)}, f32[32,1,128]{2,1,0:T(1,128)}, u32[]{:S(2)}) copy-start(f32[32,1,128]{2,1,0:T(1,128)} %param.27) | copy-start | bytes 49156
  40.4 2.3 %copy-start.47 = (bf16[4,256]{1,0:T(4,128)(2,1)S(1)}, bf16[4,256]{1,0:T(4,128)(2,1)}, u32[]{:S(2)}) copy-start(bf16[4,256]{1,0:T(4,128)(2,1)} %tb.5) | copy-start | bytes 6148
  40.4 2.3 %copy-start.50 = (bf16[4,256]{1,0:T(4,128)(2,1)S(1)}, bf16[4,256]{1,0:T(4,128)(2,1)}, u32[]{:S(2)}) copy-start(bf16[4,256]{1,0:T(4,128)(2,1)} %tc.5) | copy-start | bytes 6148
  40.4 2.3 %copy-start.53 = (s32[1,128]{1,0:T(1,128)S(1)}, s32[1,128]{1,0:T(1,128)}, u32[]{:S(2)}) copy-start(s32[1,128]{1,0:T(1,128)} %mask_ref.5) | copy-start | bytes 1540
  40.5 15.5 %collective-permute-start.4 = (s16[128,1024]{1,0:T(8,128)(2,1)S(1)}, s16[128,1024]{1,0:T(8,128)(2,1)}, u32[]{:S(2)}, u32[]{:S(2)}) collective-permute-start(s16[128,1024]{1,0:T(8,128)(2,1)S(1)} %round-nearest-even_convert_fusion.1), channel_id=1, source_target_pairs={{0,8},{4,12},{8,0},{12,4},{1,9},{5,13},{9,1},{13,5},{2,10},{6,14},... | collective-permute-start | bytes 786440 | tf_op jit(solution)/shard_map/ppermute | solution.py:449
  41.4 14.0 %collective-permute-start.9 = (f32[3,1024]{1,0:T(4,128)S(1)}, f32[3,1024]{1,0:T(4,128)S(1)}, u32[]{:S(2)}, u32[]{:S(2)}) collective-permute-start(f32[3,1024]{1,0:T(4,128)S(1)} %collective-permute-done.8), channel_id=1, source_target_pairs={{0,4},{4,0},{8,12},{12,8},{1,5},{5,1},{9,13},{13,9},{2,6},{6,2},{1... | collective-permute-start | bytes 36872 | tf_op jit(solution)/shard_map/ppermute | solution.py:449
  56.0 3.3 %collective-permute-start.7 = (s16[128,1024]{1,0:T(8,128)(2,1)}, s16[128,1024]{1,0:T(8,128)(2,1)}, u32[]{:S(2)}, u32[]{:S(2)}) collective-permute-start(s16[128,1024]{1,0:T(8,128)(2,1)} %collective-permute-done.6), channel_id=1, source_target_pairs={{0,4},{4,0},{8,12},{12,8},{1,5},{5,1},{9,13},{13,9},{2,6},{6,2},{1... | collective-permute-start | bytes 786440 | tf_op jit(solution)/shard_map/ppermute | solution.py:449
  56.0 4.7 %collective-permute-start.5 = (s16[128,1024]{1,0:T(8,128)(2,1)}, s16[128,1024]{1,0:T(8,128)(2,1)}, u32[]{:S(2)}, u32[]{:S(2)}) collective-permute-start(s16[128,1024]{1,0:T(8,128)(2,1)} %collective-permute-done.4), channel_id=1, source_target_pairs={{0,4},{4,0},{8,12},{12,8},{1,5},{5,1},{9,13},{13,9},{2,6},{6,2},{1... | collective-permute-start | bytes 786440 | tf_op jit(solution)/shard_map/ppermute | solution.py:449
  (37 other events, 39.4 us)

commit v2 on v1

--- a/solution.py
+++ b/solution.py
@@ -80,11 +80,20 @@
     return ((col >= row * HD) & (col < (row + 1) * HD)).astype(F32)
 
 
+def column(row_ref, heads):
+    shape = (heads, row_ref.shape[1])
+    row = lax.broadcasted_iota(jnp.int32, shape, 0) + pl.program_id(0) * heads
+    col = lax.broadcasted_iota(jnp.int32, shape, 1)
+    return jnp.sum(jnp.where(row == col, row_ref[...], 0.0), axis=1, keepdims=True)
+
+
 def decays(dt_ref, bias_ref, rate_ref):
-    raw = dt_ref[...] + bias_ref[...]
+    heads = dt_ref.shape[0]
+    rate = column(rate_ref, heads)
+    raw = dt_ref[...] + column(bias_ref, heads)
     step = softplus(raw)
     cum = lax.dot_general(
-        -step * rate_ref[...], tri().astype(F32), NN, precision=EXACT, preferred_element_type=F32
+        -step * rate, tri().astype(F32), NN, precision=EXACT, preferred_element_type=F32
     )
     return raw, step, cum
 
@@ -202,7 +211,9 @@
     pull = jnp.exp(cum)
     if weight is not None:
         pull = pull * weight
-    gain = skip[...] if weight is None else skip[...] * weight
+    gain = column(skip, heads)
+    if weight is not None:
+        gain = gain * weight
     gain = jnp.broadcast_to(gain, (heads, Q))
     last = cum[:, Q - 1 : Q]
     push = jnp.exp(last - cum) * step
@@ -267,7 +278,7 @@
     dlog = end + lax.dot_general(
         change, tri(True).astype(F32), NN, precision=EXACT, preferred_element_type=F32
     )
-    ddt[...] = (cols_t / step - rate[...] * dlog) * jax.nn.sigmoid(raw)
+    ddt[...] = (cols_t / step - column(rate, heads) * dlog) * jax.nn.sigmoid(raw)
 
 
 def carried_kernel(
@@ -275,7 +286,7 @@
     px, pb, pc, pdt, pg, phx, phb, phc,
     sx, sb, sc, sdt, sg, shx, shb, shc,
     tx, tb, tc, rate, bias, skip,
-    start, own, tail, suf, own_q, sec_q, rows,
+    start, own, tail, suf, own_got, sec_got, own_other, sec_other, rows,
     p_idx, p_idb, p_idc, p_r, s_idx, s_idb, s_idc, s_r,
     p_dx, p_db, p_dc, p_ddt, s_dx, s_db, s_dc, s_ddt,
     lx, lb, lc, ptx, ptb, ptc,
@@ -283,15 +294,21 @@
     for left in (lx, lb, lc):
         left[...] = jnp.zeros_like(left)
 
+    def pick(got, other, cols):
+        at = cols.start % got.shape[1]
+        half = slice(at, at + cols.stop - cols.start)
+        here = rows[7:8, cols] > 0.5
+        return jnp.where(here, got[:, half].astype(F32), other[:, half].astype(F32))
+
     def prompt_state(cols):
-        other = own_q[:, cols].astype(F32)
-        second = sec_q[:, cols].astype(F32)
-        begin = start[:, cols] + rows[0:1, cols] * other
-        adjoint = tail[:, cols] + rows[3:4, cols] * second + rows[4:5, cols] * suf[:, cols]
-        return begin, adjoint
+        other = pick(own_got, own_other, cols)
+        second = pick(sec_got, sec_other, cols)
+        begin = rows[5:6, cols] * start[:, cols] + rows[0:1, cols] * other
+        adjoint = rows[6:7, cols] * tail[:, cols] + rows[3:4, cols] * second
+        return begin, adjoint + rows[4:5, cols] * suf[:, cols]
 
     def suffix_state(cols):
-        other = own_q[:, cols].astype(F32)
+        other = pick(own_got, own_other, cols)
         return rows[1:2, cols] * own[:, cols] + rows[2:3, cols] * other, None
 
     carried(px, pb, pc, pdt, pg, phx, phb, phc, tx, tb, tc, rate, bias, skip, None,
@@ -323,9 +340,10 @@
     pl.semaphore_wait(barrier, ways - 1)
 
 
-def halo_kernel(ways, x_ref, out_ref, send, recv):
+def halo_kernel(ways, tx, tb, tc, out_ref, x_ref, send, recv):
     me = lax.axis_index("suf")
     last = ways - 1
+    x_ref[...] = jnp.concatenate([tx[...], tb[...], tc[...]], axis=1)
     greet(ways, me)
     right = remote(x_ref, out_ref.at[0], send.at[last], recv.at[0], lax.rem(me + 1, ways))
     spread = [remote(x_ref, out_ref.at[1], send.at[i], recv.at[1], i) for i in range(last)]
@@ -356,21 +374,30 @@
         right.wait_recv()
 
 
-def halo(block, ways):
+def halo(sources, ways):
+    width = sum(source.shape[1] for source in sources)
     return pl.pallas_call(
         functools.partial(halo_kernel, ways),
-        out_shape=jax.ShapeDtypeStruct((2,) + block.shape, block.dtype),
-        in_specs=[pl.BlockSpec(memory_space=pltpu.VMEM)],
+        grid=(1,),
+        out_shape=jax.ShapeDtypeStruct((2, 16, width), BF16),
+        in_specs=[
+            pl.BlockSpec((16, source.shape[1]), lambda i: (Q // 16 - 1, 0)) for source in sources
+        ],
         out_specs=pl.BlockSpec(memory_space=pltpu.VMEM),
-        scratch_shapes=[pltpu.SemaphoreType.DMA((ways,)), pltpu.SemaphoreType.DMA((2,))],
+        scratch_shapes=[
+            pltpu.VMEM((16, width), BF16),
+            pltpu.SemaphoreType.DMA((ways,)),
+            pltpu.SemaphoreType.DMA((2,)),
+        ],
         compiler_params=pltpu.CompilerParams(collective_id=0, has_side_effects=True),
         name="halo",
-    )(block)
-
-
-def sum_kernel(ways, x_ref, out_ref, slots, send, recv):
+    )(*sources)
+
+
+def sum_kernel(ways, lx, lb, lc, out_ref, x_ref, slots, send, recv):
     me = lax.axis_index("suf")
     last = ways - 1
+    x_ref[...] = jnp.concatenate([lx[...], lb[...], lc[...]], axis=1)
     greet(ways, me)
     left = remote(x_ref, slots.at[last], send.at[0], recv.at[last], lax.rem(me + last, ways))
     up = remote(x_ref, slots.at[me], send.at[1], recv.at[me], last)
@@ -402,20 +429,22 @@
         out_ref[0:3] = total
 
 
-def sum_rows(block, ways):
+def sum_rows(sources, ways):
+    shape = (8, sum(source.shape[1] for source in sources))
     return pl.pallas_call(
         functools.partial(sum_kernel, ways),
-        out_shape=jax.ShapeDtypeStruct(block.shape, block.dtype),
-        in_specs=[pl.BlockSpec(memory_space=pltpu.VMEM)],
+        out_shape=jax.ShapeDtypeStruct(shape, F32),
+        in_specs=[pl.BlockSpec(memory_space=pltpu.VMEM)] * 3,
         out_specs=pl.BlockSpec(memory_space=pltpu.VMEM),
         scratch_shapes=[
-            pltpu.VMEM((ways,) + block.shape, block.dtype),
+            pltpu.VMEM(shape, F32),
+            pltpu.VMEM((ways,) + shape, F32),
             pltpu.SemaphoreType.DMA((2,)),
             pltpu.SemaphoreType.DMA((ways,)),
         ],
         compiler_params=pltpu.CompilerParams(collective_id=1, has_side_effects=True),
         name="sum_rows",
-    )(block)
+    )(*sources)
 
 
 def fix_kernel(extra, tx, tb, tc, dx, db, dc, ox, ob, oc):
@@ -458,17 +487,22 @@
 
 def combine(own, adj, suf, dec, ways):
     me = lax.axis_index("suf")
-    start = jnp.zeros_like(own)
-    before = jnp.ones_like(dec)
-    tail = jnp.zeros_like(adj)
-    after = jnp.ones_like(dec)
+    one = jnp.ones_like(dec)
+    zero = jnp.zeros_like(dec)
+    before, after, start = one, one, None
     bit = 1
     while bit * 2 < ways:
         upper = (me & bit) != 0
         own_, adj_, suf_, dec_ = exchange((own, adj, suf, dec), bit, ways)
-        start = jnp.where(upper, before * own_ + start, start)
+        if start is None:
+            start, tail = own_, adj_
+            start_by, tail_by = jnp.where(upper, one, zero), jnp.where(upper, zero, one)
+        else:
+            start, tail = start_by * start, tail_by * tail
+            start = jnp.where(upper, before * own_ + start, start)
+            tail = jnp.where(upper, tail, tail + after * adj_)
+            start_by, tail_by = one, one
         before = jnp.where(upper, before * dec_, before)
-        tail = jnp.where(upper, tail, tail + after * adj_)
         after = jnp.where(upper, after, after * dec_)
         own = jnp.where(upper, dec * own_ + own, dec_ * own + own_)
         adj = jnp.where(upper, adj_ + dec_ * adj, adj + dec * adj_)
@@ -491,18 +525,20 @@
     def whole(a, b):
         return jnp.where(core == 0, jnp.concatenate([a, b], 1), jnp.concatenate([b, a], 1))
 
-    own_q, sec_q, small = [whole(a, b) for a, b in zip(got, other)]
+    small = whole(got[2], other[2])
     own_s, sec_s, dec_ = small[0:1], small[1:2], small[2:3]
-    zero = jnp.zeros_like(dec)
+    here = lax.broadcasted_iota(jnp.int32, dec.shape, 1) // half == core
     rows = [
         jnp.where(upper, before, zero) * own_s,
-        jnp.where(upper, jnp.ones_like(dec), dec_),
-        jnp.where(upper, dec, jnp.ones_like(dec)) * own_s,
+        jnp.where(upper, one, dec_),
+        jnp.where(upper, dec, one) * own_s,
         after * sec_s,
         jnp.where(upper, after, after * dec_),
-        zero, zero, zero,
+        start_by,
+        tail_by,
+        here.astype(F32),
     ]
-    return start, own, tail, suf, own_q, sec_q, jnp.concatenate(rows, axis=0)
+    return start, own, tail, suf, *got[:2], *other[:2], jnp.concatenate(rows, axis=0)
 
 
 def shards(
@@ -518,8 +554,7 @@
     full = heads * HD
     nb = groups * N
 
-    tails = jnp.concatenate([prefix_x[-16:], prefix_b[-16:], prefix_c[-16:]], axis=1)
-    halos = halo(tails, ways)
+    halos = halo((prefix_x, prefix_b, prefix_c), ways)
 
     def halo_specs(slot):
         def at(width, first):
@@ -535,7 +570,7 @@
     hb = pl.BlockSpec((8, N), lambda g: (0, g))
     kx = pl.BlockSpec((KW, wide), lambda g: (0, g))
     kb = pl.BlockSpec((KW, N), lambda g: (0, g))
-    ph = pl.BlockSpec((per, 1), lambda g: (g, 0))
+    ph = pl.BlockSpec((1, heads), lambda g: (0, 0))
     half = [sx, sb, sb, sdt, sx]
     base_specs = (
         [sm, sm, pl.BlockSpec((1, Q), lambda g: (0, 0))] + half + halo_specs(0) + half + halo_specs(1) + [kx, kb, kb, ph, ph, ph]
@@ -546,13 +581,16 @@
         + (halos,) * 3
         + (suffix_x[0], suffix_b[0], suffix_c[0], suffix_dt[:, 0], suffix_grad[0])
         + (halos,) * 3
-        + (conv_x, conv_b, conv_c, decay_rate[:, None], dt_bias[:, None], skip[:, None])
+        + (conv_x, conv_b, conv_c, decay_rate[None], dt_bias[None], skip[None])
     )
 
     def shape(rows, columns, kind=F32):
         return jax.ShapeDtypeStruct((rows, columns), kind)
 
-    params = pltpu.CompilerParams(vmem_limit_bytes=48 * 1024 * 1024)
+    half_width = full // 2
+    sq_width = min(wide, half_width)
+    sq = pl.BlockSpec((N, sq_width), lambda g: (0, lax.rem(g, half_width // sq_width)))
+    params = pltpu.CompilerParams(vmem_limit_bytes=60 * 1024 * 1024)
     state_shape = shape(N, full)
     own, adj, suf, dec = pl.pallas_call(
         states_kernel,
@@ -587,14 +625,14 @@
     outs = pl.pallas_call(
         carried_kernel,
         grid=(groups,),
-        in_specs=base_specs + [sx] * 6 + [hx] + inner_specs * 2,
+        in_specs=base_specs + [sx] * 4 + [sq] * 4 + [hx] + inner_specs * 2,
         out_specs=out_specs,
         out_shape=out_shape,
         compiler_params=params,
         name="carried",
     )(*base, *states, *inner)
 
-    extra = sum_rows(jnp.concatenate(outs[8:11], axis=1), ways)
+    extra = sum_rows(outs[8:11], ways)
     finished = fix(extra, outs[11:14], outs[:3])
     return (
         *finished,

time: 88.3 us -> 66.7 us (0.76)
  local copies, waits for them, and re-layouts: 21.6 us -> 2.32 us
  other arithmetic: 9.87 us -> 4.82 us
  Pallas kernels: 43.1 us -> 46.9 us
  waiting for transfers between devices: 4.97 us -> 3.67 us
  starting transfers between devices: 5.23 us -> 6.4 us
    unnamed x116 -> x14, local copies, waits for them, and re-layouts: 15.8 us -> 0.74 us
    select_n x3 -> x1, other arithmetic: 2.81 us -> 0.01 us  [whole(): jnp.where(core == 0, jnp.concatenate([a, b], 1), jnp.concatenate([b, a], 1))]
    broadcast_in_dim x3 -> x0, local copies, waits for them, and re-layouts: 2.25 us -> none  [the longest x1 0.75 us: shards(): dt_bias[:, None]]
    pallas_call x1, Pallas kernels: 8.03 us -> 9.57 us  [shards(): pl.pallas_call(within_kernel, grid=(groups,), in_specs=base_specs, out_sp...]
    slice x4 -> x0, local copies, waits for them, and re-layouts: 1.46 us -> none  [the longest x1 0.76 us: shards(): prefix_b[-16:]]
    concatenate x2 -> x1, local copies, waits for them, and re-layouts: 2.16 us -> 0.72 us  [combine(): jnp.concatenate(rows, axis=0)]
    ppermute x10, waiting for transfers between devices: 4.97 us -> 3.67 us  [exchange(): return [lax.ppermute(part, 'suf', route) for part in parts]]
    concatenate x2 -> x0, other arithmetic: 1.28 us -> none  [the longest x1 0.64 us: shards(): jnp.concatenate([prefix_x[-16:], prefix_b[-16:], prefix_c[-16:]], axis=1)]
  transfers between devices with their start and end apart: 10 -> 10, of which waited for: 4 -> 4; matrix products, arithmetic and copies ran while one was open for 5% -> 4% of each run, Pallas kernels for 9% -> 14%
where the time goes in v2:
time: 66.7 us; the launch traced here: 66.3 us
  Pallas kernels  46.9 us (70%)
  starting transfers between devices  6.4 us (10%)
  other arithmetic  4.82 us (7%)
  waiting for transfers between devices  3.67 us (6%)
  local copies, waits for them, and re-layouts  2.32 us (3%)
  between operations  2.14 us (3%)
    pallas_call x1, Pallas kernels, shards(): pl.pallas_call(carried_kernel, grid=(groups,), in_specs=base_specs + [sx]...  15.9 us
    pallas_call x1, Pallas kernels, shards(): pl.pallas_call(within_kernel, grid=(groups,), in_specs=base_specs, out_sp...  9.57 us
    pallas_call x1, Pallas kernels, shards(): pl.pallas_call(states_kernel, grid=(groups,), in_specs=base_specs, out_sp...  7.13 us
    pallas_call x1, Pallas kernels, halo(): pl.pallas_call(functools.partial(halo_kernel, ways), grid=(1,), out_shape...  7.04 us
    ppermute x10, starting transfers between devices, exchange(): return [lax.ppermute(part, 'suf', route) for part in parts]  6.4 us
    pallas_call x1, Pallas kernels, sum_rows(): pl.pallas_call(functools.partial(sum_kernel, ways), out_shape=jax.ShapeDt...  5.68 us
    ppermute x10, waiting for transfers between devices, exchange(): return [lax.ppermute(part, 'suf', route) for part in parts]  3.67 us
    select_n x1, other arithmetic, combine(): second = jnp.where(upper, adj + dec * suf, suf)  3.54 us
  transfers between devices with their start and end apart: 10, of which 4 were waited for; matrix products, arithmetic and copies ran while one was open for 4% of the time, Pallas kernels for 14%

profile of v2, /device:TPU:1, one launch (start us, length us, event | category | flops | bytes accessed | tf_op | source)
XLA Modules:
  0.0 66.3 jit_solution(14163697774080117997)
XLA Ops:
  1.9 7.0 %halo.1.phx.phb.phc.shx.shb.shc = bf16[2,16,2560]{2,1,0:T(8,128)(2,1)} custom-call(bf16[128,2048]{1,0:T(8,128)(2,1)} %px.5, bf16[128,256]{1,0:T(8,128)(2,1)} %pb.5, bf16[128,256]{1,0:T(8,128)(2,1)} %pc.5), custom_call_target="tpu_custom_call" | custom-call | tf_op jit(solution)/shard_map/halo/pallas_call | solution.py:379
  9.0 7.1 %states.1 = (f32[128,2048]{1,0:T(8,128)}, f32[128,2048]{1,0:T(8,128)}, f32[128,2048]{1,0:T(8,128)}, f32[8,2048]{1,0:T(8,128)}) custom-call(s32[1]{0:T(128)S(6)} %copy.34.len_ref, f32[1]{0:T(128)S(6)} %copy.35.adv_ref, s32[1,128]{1,0:T(1,128)} %mask_ref.5, bf16[128,2048]{1,0:T(8,128)(2,1)} %px.5, bf16[128,256]{1,0:T(8,128)(2,1)} %pb.5, bf16[128,256]{1,0:T(8,128)(2,1)} %pc.5, ...), custom_call_target="tpu_custom_call" | custom-call | tf_op jit(solution)/shard_map/states/pallas_call | solution.py:595
  16.1 0.1 collective-permute-start
  16.2 0.5 collective-permute-start.2
  16.7 0.1 collective-permute-start.3
  16.8 0.8 %slice.30 = f32[1,2048]{1,0:T(1,128)S(1)} slice(f32[8,2048]{1,0:T(8,128)} %get-tuple-element.38), slice={[0:1], [0:2048]} | slice | bytes 16384 | tf_op jit(solution)/shard_map/slice | solution.py:620
  17.6 0.4 collective-permute-start.1
  18.1 1.9 %collective-permute-done.1 = f32[1,2048]{1,0:T(1,128)S(1)} collective-permute-done((f32[1,2048]{1,0:T(1,128)S(1)}, f32[1,2048]{1,0:T(1,128)S(1)}, u32[]{:S(2)}, u32[]{:S(2)}) %collective-permute-start.1) | collective-permute-done | bytes 8224 | tf_op jit(solution)/shard_map/ppermute | solution.py:478
  20.0 0.8 %slice_multiply_fusion.1 = f32[1,2048]{1,0:T(1,128)S(1)} fusion(f32[1,2048]{1,0:T(1,128)S(1)} %collective-permute-done.1, f32[8,2048]{1,0:T(8,128)} %get-tuple-element.38), kind=kLoop, calls=%fused_computation.33 | loop fusion | flops 2048 | bytes 24576 | tf_op jit(solution)/shard_map/mul | solution.py:510
  20.8 0.0 collective-permute-done.start
  20.9 1.2 %collective-permute-done.3 = f32[128,2048]{1,0:T(8,128)S(1)} collective-permute-done((f32[128,2048]{1,0:T(8,128)}, f32[128,2048]{1,0:T(8,128)S(1)}, u32[]{:S(2)}, u32[]{:S(2)}) %collective-permute-start.3) | collective-permute-done | bytes 1048608 | tf_op jit(solution)/shard_map/ppermute | solution.py:478
  22.1 3.5 %add_select_fusion = (f32[128,2048]{1,0:T(8,128)S(1)}, f32[128,2048]{1,0:T(8,128)}, f32[128,2048]{1,0:T(8,128)S(1)}) fusion(f32[128,2048]{1,0:T(8,128)} %get-tuple-element.39, f32[128,2048]{1,0:T(8,128)S(1)} %collective-permute-done.2.tail, f32[2048]{0:T(1024)S(1)} %bitcast.31, f32[2048]{0:T(1024)S(1)} %bitcast.32, f32[2048]{0:T(1024)S(1)} %bitcast.36, ...), kind=kLoop, calls=%fused_computation | loop fusion | flops 3670016 | bytes 9461762 | tf_op jit(solution)/shard_map/jit(_where)/select_n | solution.py:519
  25.6 0.1 abs_reduce_fusion
  25.7 0.1 abs_reduce_fusion.1
  25.8 0.9 %collective-permute-start.8 = (f32[3,1024]{1,0:T(4,128)S(1)}, f32[3,1024]{1,0:T(4,128)S(1)}, u32[]{:S(2)}, u32[]{:S(2)}) collective-permute-start(f32[3,1024]{1,0:T(4,128)S(1)} %pad_maximum_fusion), channel_id=1, source_target_pairs={{0,8},{4,12},{8,0},{12,4},{1,9},{5,13},{9,1},{13,5},{2,10},{6,14},... | collective-permute-start | bytes 36872 | tf_op jit(solution)/shard_map/ppermute | solution.py:478
  26.7 0.1 round-nearest-even_convert_fusion
  26.8 0.7 %collective-permute-start.5 = (s16[128,1024]{1,0:T(8,128)(2,1)S(1)}, s16[128,1024]{1,0:T(8,128)(2,1)S(1)}, u32[]{:S(2)}, u32[]{:S(2)}) collective-permute-start(s16[128,1024]{1,0:T(8,128)(2,1)S(1)} %round-nearest-even_convert_fusion), channel_id=1, source_target_pairs={{0,8},{4,12},{8,0},{12,4},{1,9},{5,13},{9,1},{13,5},{2,10},{6,14},... | collective-permute-start | bytes 786440 | tf_op jit(solution)/shard_map/ppermute | solution.py:478
  27.5 0.1 round-nearest-even_convert_fusion.1
  27.6 0.9 %collective-permute-start.4 = (s16[128,1024]{1,0:T(8,128)(2,1)S(1)}, s16[128,1024]{1,0:T(8,128)(2,1)S(1)}, u32[]{:S(2)}, u32[]{:S(2)}) collective-permute-start(s16[128,1024]{1,0:T(8,128)(2,1)S(1)} %round-nearest-even_convert_fusion.1), channel_id=1, source_target_pairs={{0,8},{4,12},{8,0},{12,4},{1,9},{5,13},{9,1},{13,5},{2,10},{6,14},... | collective-permute-start | bytes 786440 | tf_op jit(solution)/shard_map/ppermute | solution.py:478
  28.5 0.0 collective-permute-done.8
  28.5 1.2 %collective-permute-start.9 = (f32[3,1024]{1,0:T(4,128)S(1)}, f32[3,1024]{1,0:T(4,128)S(1)}, u32[]{:S(2)}, u32[]{:S(2)}) collective-permute-start(f32[3,1024]{1,0:T(4,128)S(1)} %collective-permute-done.8), channel_id=1, source_target_pairs={{0,4},{4,0},{8,12},{12,8},{1,5},{5,1},{9,13},{13,9},{2,6},{6,2},{1... | collective-permute-start | bytes 36872 | tf_op jit(solution)/shard_map/ppermute | solution.py:478
  29.7 9.6 %within.1 = (f32[128,2048]{1,0:T(8,128)}, f32[128,256]{1,0:T(8,128)}, f32[128,256]{1,0:T(8,128)}, f32[32,128]{1,0:T(8,128)}, f32[128,2048]{1,0:T(8,128)}, /*inde...) custom-call(s32[1]{0:T(128)S(6)} %copy.34.len_ref, f32[1]{0:T(128)S(6)} %copy.35.adv_ref, s32[1,128]{1,0:T(1,128)} %mask_ref.5, ...), custom_call_target="tpu_custom_call" | custom-call | flops 1610612736 | bytes 6291456 | tf_op jit(solution)/shard_map/within/pallas_call | solution.py:607
  39.4 0.1 collective-permute-start.7
  39.4 0.2 collective-permute-done.4.own_got
  39.7 1.5 %collective-permute-start.6 = (s16[128,1024]{1,0:T(8,128)(2,1)S(1)}, s16[128,1024]{1,0:T(8,128)(2,1)S(1)}, u32[]{:S(2)}, u32[]{:S(2)}) collective-permute-start(s16[128,1024]{1,0:T(8,128)(2,1)S(1)} %collective-permute-done.4.own_got), channel_id=1, source_target_pairs={{0,4},{4,0},{8,12},{12,8},{1,5},{5,1},{9,13},{13,9},{2,6},{6,2},{1... | collective-permute-start | bytes 786440 | tf_op jit(solution)/shard_map/ppermute | solution.py:478
  41.3 0.7 %concatenate.15.rows = f32[8,2048]{1,0:T(8,128)} concatenate(f32[1,2048]{1,0:T(1,128)S(1)} %get-tuple-element.78, f32[1,2048]{1,0:T(1,128)S(1)} %get-tuple-element.79, f32[1,2048]{1,0:T(1,128)S(1)} %get-tuple-element.80, f32[1,2048]{1,0:T(1,128)S(1)} %get-tuple-element.77, f32[1,2048]{1,0:T(1,128)S(1)} %get-tuple-element.76, f32[1,2048]{1,0:T(1,128)S(1)} %select_n.161, ...), dimensions={0} | concatenate | bytes 131072 | tf_op jit(solution)/shard_map/concatenate | solution.py:541
  42.0 0.4 collective-permute-done.6.own_other
  42.4 0.3 copy-done.5
  42.7 0.4 copy-done.6
  43.1 15.9 %carried.1 = (bf16[128,2048]{1,0:T(8,128)(2,1)}, bf16[128,256]{1,0:T(8,128)(2,1)}, bf16[128,256]{1,0:T(8,128)(2,1)}, f32[32,128]{1,0:T(8,128)}, bf16[128,2048]{1...) custom-call(s32[1]{0:T(128)S(6)} %copy.34.len_ref, ...), custom_call_target="tpu_custom_call" | custom-call | tf_op jit(solution)/shard_map/carried/pallas_call | solution.py:625
  59.0 5.7 %sum_rows.1.extra = f32[8,2560]{1,0:T(8,128)} custom-call(f32[8,2048]{1,0:T(8,128)} %get-tuple-element.49.lx, f32[8,256]{1,0:T(8,128)} %get-tuple-element.50.lb, f32[8,256]{1,0:T(8,128)} %get-tuple-element.51.lc), custom_call_target="tpu_custom_call" | custom-call | tf_op jit(solution)/shard_map/sum_rows/pallas_call | solution.py:434
  64.7 1.6 %fix.1 = (bf16[128,2048]{1,0:T(8,128)(2,1)}, bf16[128,256]{1,0:T(8,128)(2,1)}, bf16[128,256]{1,0:T(8,128)(2,1)}) custom-call(f32[8,2560]{1,0:T(8,128)} %sum_rows.1.extra, f32[8,2048]{1,0:T(8,128)} %get-tuple-element.52.tx, f32[8,256]{1,0:T(8,128)} %get-tuple-element.53.tb, ...), custom_call_target="tpu_custom_call", output_to_operand_aliasing={{0}: (4, {}), {1}: (5, {}), {2}: (6, {})} | custom-call | tf_op jit(solution)/shard_map/fix/pallas_call | solution.py:465
  (25 shorter events, 0.2 us)
Async XLA Ops:
  16.1 4.7 %collective-permute-start = (f32[128,2048]{1,0:T(8,128)}, f32[128,2048]{1,0:T(8,128)S(1)}, u32[]{:S(2)}, u32[]{:S(2)}) collective-permute-start(f32[128,2048]{1,0:T(8,128)} %get-tuple-element.37), channel_id=1, source_target_pairs={{0,4},{4,0},{8,12},{12,8},{1,5},{5,1},{9,13},{13,9},{2,6},{6,2},{1... | collective-permute-start | bytes 3145736 | tf_op jit(solution)/shard_map/ppermute | solution.py:478
  16.2 4.7 %collective-permute-start.2 = (f32[128,2048]{1,0:T(8,128)}, f32[128,2048]{1,0:T(8,128)S(1)}, u32[]{:S(2)}, u32[]{:S(2)}) collective-permute-start(f32[128,2048]{1,0:T(8,128)} %get-tuple-element.39), channel_id=1, source_target_pairs={{0,4},{4,0},{8,12},{12,8},{1,5},{5,1},{9,13},{13,9},{2,6},{6,2},{1... | collective-permute-start | bytes 3145736 | tf_op jit(solution)/shard_map/ppermute | solution.py:478
  16.7 5.4 %collective-permute-start.3 = (f32[128,2048]{1,0:T(8,128)}, f32[128,2048]{1,0:T(8,128)S(1)}, u32[]{:S(2)}, u32[]{:S(2)}) collective-permute-start(f32[128,2048]{1,0:T(8,128)} %get-tuple-element.40), channel_id=1, source_target_pairs={{0,4},{4,0},{8,12},{12,8},{1,5},{5,1},{9,13},{13,9},{2,6},{6,2},{1... | collective-permute-start | bytes 3145736 | tf_op jit(solution)/shard_map/ppermute | solution.py:478
  17.6 2.4 %collective-permute-start.1 = (f32[1,2048]{1,0:T(1,128)S(1)}, f32[1,2048]{1,0:T(1,128)S(1)}, u32[]{:S(2)}, u32[]{:S(2)}) collective-permute-start(f32[1,2048]{1,0:T(1,128)S(1)} %slice.30), channel_id=1, source_target_pairs={{0,4},{4,0},{8,12},{12,8},{1,5},{5,1},{9,13},{13,9},{2,6},{6,2},{1... | collective-permute-start | bytes 24584 | tf_op jit(solution)/shard_map/ppermute | solution.py:478
  20.9 4.7 %copy-start.1 = (f32[128,2048]{1,0:T(8,128)}, f32[128,2048]{1,0:T(8,128)S(1)}, u32[]{:S(2)}) copy-start(f32[128,2048]{1,0:T(8,128)S(1)} %collective-permute-done.start) | copy-start | bytes 3145732
  20.9 4.7 %copy-start.2 = (f32[128,2048]{1,0:T(8,128)}, f32[128,2048]{1,0:T(8,128)S(1)}, u32[]{:S(2)}) copy-start(f32[128,2048]{1,0:T(8,128)S(1)} %collective-permute-done.2.tail) | copy-start | bytes 3145732
  25.6 1.9 %copy-start = (f32[128,2048]{1,0:T(8,128)}, f32[128,2048]{1,0:T(8,128)S(1)}, u32[]{:S(2)}) copy-start(f32[128,2048]{1,0:T(8,128)S(1)} %get-tuple-element.81.own) | copy-start | bytes 3145732
  25.8 2.7 %collective-permute-start.8 = (f32[3,1024]{1,0:T(4,128)S(1)}, f32[3,1024]{1,0:T(4,128)S(1)}, u32[]{:S(2)}, u32[]{:S(2)}) collective-permute-start(f32[3,1024]{1,0:T(4,128)S(1)} %pad_maximum_fusion), channel_id=1, source_target_pairs={{0,8},{4,12},{8,0},{12,4},{1,9},{5,13},{9,1},{13,5},{2,10},{6,14},... | collective-permute-start | bytes 36872 | tf_op jit(solution)/shard_map/ppermute | solution.py:478
  26.8 12.6 %collective-permute-start.5 = (s16[128,1024]{1,0:T(8,128)(2,1)S(1)}, s16[128,1024]{1,0:T(8,128)(2,1)S(1)}, u32[]{:S(2)}, u32[]{:S(2)}) collective-permute-start(s16[128,1024]{1,0:T(8,128)(2,1)S(1)} %round-nearest-even_convert_fusion), channel_id=1, source_target_pairs={{0,8},{4,12},{8,0},{12,4},{1,9},{5,13},{9,1},{13,5},{2,10},{6,14},... | collective-permute-start | bytes 786440 | tf_op jit(solution)/shard_map/ppermute | solution.py:478
  27.6 12.1 %collective-permute-start.4 = (s16[128,1024]{1,0:T(8,128)(2,1)S(1)}, s16[128,1024]{1,0:T(8,128)(2,1)S(1)}, u32[]{:S(2)}, u32[]{:S(2)}) collective-permute-start(s16[128,1024]{1,0:T(8,128)(2,1)S(1)} %round-nearest-even_convert_fusion.1), channel_id=1, source_target_pairs={{0,8},{4,12},{8,0},{12,4},{1,9},{5,13},{9,1},{13,5},{2,10},{6,14},... | collective-permute-start | bytes 786440 | tf_op jit(solution)/shard_map/ppermute | solution.py:478
  28.5 10.8 %collective-permute-start.9 = (f32[3,1024]{1,0:T(4,128)S(1)}, f32[3,1024]{1,0:T(4,128)S(1)}, u32[]{:S(2)}, u32[]{:S(2)}) collective-permute-start(f32[3,1024]{1,0:T(4,128)S(1)} %collective-permute-done.8), channel_id=1, source_target_pairs={{0,4},{4,0},{8,12},{12,8},{1,5},{5,1},{9,13},{13,9},{2,6},{6,2},{1... | collective-permute-start | bytes 36872 | tf_op jit(solution)/shard_map/ppermute | solution.py:478
  39.4 3.0 %copy-start.3 = (s16[128,1024]{1,0:T(8,128)(2,1)}, s16[128,1024]{1,0:T(8,128)(2,1)S(1)}, u32[]{:S(2)}) copy-start(s16[128,1024]{1,0:T(8,128)(2,1)S(1)} %collective-permute-done.5.sec_got) | copy-start | bytes 786436
  39.4 2.6 %collective-permute-start.7 = (s16[128,1024]{1,0:T(8,128)(2,1)S(1)}, s16[128,1024]{1,0:T(8,128)(2,1)S(1)}, u32[]{:S(2)}, u32[]{:S(2)}) collective-permute-start(s16[128,1024]{1,0:T(8,128)(2,1)S(1)} %collective-permute-done.5.sec_got), channel_id=1, source_target_pairs={{0,4},{4,0},{8,12},{12,8},{1,5},{5,1},{9,13},{13,9},{2,6},{6,2},{1... | collective-permute-start | bytes 786440 | tf_op jit(solution)/shard_map/ppermute | solution.py:478
  39.7 2.7 %copy-start.4 = (s16[128,1024]{1,0:T(8,128)(2,1)}, s16[128,1024]{1,0:T(8,128)(2,1)S(1)}, u32[]{:S(2)}) copy-start(s16[128,1024]{1,0:T(8,128)(2,1)S(1)} %collective-permute-done.4.own_got) | copy-start | bytes 786436
  39.7 2.7 %collective-permute-start.6 = (s16[128,1024]{1,0:T(8,128)(2,1)S(1)}, s16[128,1024]{1,0:T(8,128)(2,1)S(1)}, u32[]{:S(2)}, u32[]{:S(2)}) collective-permute-start(s16[128,1024]{1,0:T(8,128)(2,1)S(1)} %collective-permute-done.4.own_got), channel_id=1, source_target_pairs={{0,4},{4,0},{8,12},{12,8},{1,5},{5,1},{9,13},{13,9},{2,6},{6,2},{1... | collective-permute-start | bytes 786440 | tf_op jit(solution)/shard_map/ppermute | solution.py:478
  42.0 0.7 %copy-start.5 = (s16[128,1024]{1,0:T(8,128)(2,1)}, s16[128,1024]{1,0:T(8,128)(2,1)S(1)}, u32[]{:S(2)}) copy-start(s16[128,1024]{1,0:T(8,128)(2,1)S(1)} %collective-permute-done.7.sec_other) | copy-start | bytes 786436
  42.4 0.7 %copy-start.6 = (s16[128,1024]{1,0:T(8,128)(2,1)}, s16[128,1024]{1,0:T(8,128)(2,1)S(1)}, u32[]{:S(2)}) copy-start(s16[128,1024]{1,0:T(8,128)(2,1)S(1)} %collective-permute-done.6.own_other) | copy-start | bytes 786436
